TPU v7x, 512 devices: a whole 4x4x16 slice. The times are simulated.
512 devices in a mesh: sub: 128 (over y, z, core), grp: 4 (over x).
Axes of the slice: x: 4, y: 4, z: 16, core: 2. Of those that a mesh axis runs over, the one named last changes fastest.
Arguments:
- multipliers: float32 [512, 9, 256], P(('sub', 'grp')), may hold values from -6 to 6
- residual: float32 [512, 9, 256], P(('sub', 'grp')), may hold values from -6 to 6
- stiff_class: int32 [512, 16, 256], P(('sub', 'grp')), may hold values from 0 to 7
- moduli: float32 [8], replicated, may hold values from 1 to 30
- coarse_panel: float32 [512, 24, 96], P(('sub', 'grp')), as said below
Outputs:
- new_multipliers: float32 [512, 9, 256], P(('sub', 'grp'))
- new_residual: float32 [512, 9, 256], P(('sub', 'grp'))
Inputs may be any that keep to these rules, and one draw needn't show every extreme that they name: `coarse_panel`: for each s, the panels of the 4 subdomains s * 4 + g stacked in order of g form a symmetric positive definite matrix of 96 rows.
All inputs are finite; a program needn't handle non-finite values.
Results may differ from a plain program's by a relative error of at most 0.0003.
Values sent between devices are 32-bit elements; how exact they have to be, the bound alone decides.
A program may use at most 64 MiB of HBM per device.

v0:
```python
import jax
import jax.numpy as jnp
from jax import lax
from jax.sharding import PartitionSpec as P

SPAN = 4
ITERS = 2
POST_SWEEPS = 2
COARSE_SWEEPS = 4
CORNER_DOFS = 24


mass_weight = 0.5
damping = 0.8


def shifted(block, axis, distance):
    devices = range(lax.axis_size(axis))
    route = [(i - distance, i) for i in devices if i - distance in devices]
    return lax.ppermute(block, axis, route)


def build_operator(stiffness, mass_scale, edge_scale):
    side_nodes = stiffness.shape[0]
    plane_nodes = stiffness.shape[1]
    weight_x = edge_scale * 0.5 * (stiffness[1:] + stiffness[:-1])
    weight_y = edge_scale * 0.5 * (stiffness[:, side_nodes:] + stiffness[:, :-side_nodes])
    inner_edge = jnp.arange(plane_nodes - 1) % side_nodes < side_nodes - 1
    weight_z = jnp.where(
        inner_edge[None, :], edge_scale * 0.5 * (stiffness[:, 1:] + stiffness[:, :-1]), 0.0
    )
    mass_term = mass_scale * stiffness
    diagonal = mass_term + jnp.pad(weight_x, ((0, 1), (0, 0))) + jnp.pad(weight_x, ((1, 0), (0, 0)))
    diagonal = (
        diagonal
        + jnp.pad(weight_y, ((0, 0), (0, side_nodes)))
        + jnp.pad(weight_y, ((0, 0), (side_nodes, 0)))
    )
    diagonal = diagonal + jnp.pad(weight_z, ((0, 0), (0, 1))) + jnp.pad(weight_z, ((0, 0), (1, 0)))
    return (mass_term, weight_x, weight_y, weight_z, diagonal)


def apply_operator(operator, nodal):
    mass_term, weight_x, weight_y, weight_z, diagonal = operator
    side_nodes = mass_term.shape[0]
    flux_x = weight_x * (nodal[:, 1:] - nodal[:, :-1])
    flux_y = weight_y * (nodal[:, :, side_nodes:] - nodal[:, :, :-side_nodes])
    flux_z = weight_z * (nodal[:, :, 1:] - nodal[:, :, :-1])
    result = mass_term * nodal
    result = (
        result
        + jnp.pad(flux_x, ((0, 0), (1, 0), (0, 0)))
        - jnp.pad(flux_x, ((0, 0), (0, 1), (0, 0)))
    )
    result = (
        result
        + jnp.pad(flux_y, ((0, 0), (0, 0), (side_nodes, 0)))
        - jnp.pad(flux_y, ((0, 0), (0, 0), (0, side_nodes)))
    )
    result = (
        result
        + jnp.pad(flux_z, ((0, 0), (0, 0), (1, 0)))
        - jnp.pad(flux_z, ((0, 0), (0, 0), (0, 1)))
    )
    return result


def coarsen(values):
    leading = values.shape[:-2]
    half_nodes = values.shape[-2] // 2
    shaped = values.reshape(leading + (half_nodes, 2, half_nodes, 2, half_nodes, 2))
    summed = shaped.sum(axis=(-5, -3, -1))
    return summed.reshape(leading + (half_nodes, half_nodes * half_nodes))


def refine(values):
    leading = values.shape[:-2]
    half_nodes = values.shape[-2]
    cube = values.reshape(leading + (half_nodes, half_nodes, half_nodes))
    expanded = cube[..., :, None, :, None, :, None]
    expanded = jnp.broadcast_to(expanded, leading + (half_nodes, 2, half_nodes, 2, half_nodes, 2))
    return expanded.reshape(leading + (2 * half_nodes, 4 * half_nodes * half_nodes))


def vcycle(fine_op, coarse_op, source):
    fine_diag = fine_op[4]
    coarse_diag = coarse_op[4]
    solution = damping * source / fine_diag
    solution = solution + damping * (source - apply_operator(fine_op, solution)) / fine_diag
    defect = coarsen(source - apply_operator(fine_op, solution))
    correction = damping * defect / coarse_diag
    for sweep_index in range(COARSE_SWEEPS - 1):
        correction = (
            correction + damping * (defect - apply_operator(coarse_op, correction)) / coarse_diag
        )
    solution = solution + refine(correction)
    for sweep_index in range(POST_SWEEPS):
        solution = solution + damping * (source - apply_operator(fine_op, solution)) / fine_diag
    return solution


def corner_table(side_nodes):
    slope = jnp.arange(side_nodes).astype(jnp.float32) / (side_nodes - 1)
    return jnp.stack([1.0 - slope, slope])


def plane_table(corner_ramp):
    side_nodes = corner_ramp.shape[1]
    outer = corner_ramp[:, None, :, None] * corner_ramp[None, :, None, :]
    return outer.reshape(4, side_nodes * side_nodes)


def corner_sums(nodal, corner_ramp, corner_plane):
    summed = jnp.einsum(
        "cim,ai,pm->cap", nodal, corner_ramp, corner_plane, precision=lax.Precision.HIGHEST
    )
    return summed.reshape(CORNER_DOFS)


def corner_spread(values, corner_ramp, corner_plane):
    shaped = values.reshape(3, 2, 4)
    return jnp.einsum(
        "cap,ai,pm->cim", shaped, corner_ramp, corner_plane, precision=lax.Precision.HIGHEST
    )


def spread_faces(own_faces, lower_faces):
    plane_nodes = own_faces.shape[-1]
    side_nodes = int(round_side(plane_nodes))
    x_index = jnp.arange(side_nodes)[:, None]
    flat_index = jnp.arange(plane_nodes)[None, :]
    y_index = flat_index // side_nodes
    z_index = flat_index % side_nodes

    def along_y(faces):
        return jnp.tile(faces.reshape(3, side_nodes, side_nodes), (1, 1, side_nodes))

    def along_z(faces):
        return jnp.repeat(faces.reshape(3, side_nodes, side_nodes), side_nodes, axis=2)

    nodal = jnp.where(x_index == side_nodes - 1, own_faces[0][:, None, :], 0.0)
    nodal = nodal - jnp.where(x_index == 0, lower_faces[0][:, None, :], 0.0)
    nodal = nodal + jnp.where(y_index == side_nodes - 1, along_y(own_faces[1]), 0.0)
    nodal = nodal - jnp.where(y_index == 0, along_y(lower_faces[1]), 0.0)
    nodal = nodal + jnp.where(z_index == side_nodes - 1, along_z(own_faces[2]), 0.0)
    nodal = nodal - jnp.where(z_index == 0, along_z(lower_faces[2]), 0.0)
    return nodal


def round_side(plane_nodes):
    side_nodes = 1
    while side_nodes * side_nodes < plane_nodes:
        side_nodes = side_nodes + 1
    return side_nodes


def face_layers(nodal):
    side_nodes = nodal.shape[1]
    plane_nodes = nodal.shape[2]
    low_layer = jnp.stack(
        [
            nodal[:, 0, :],
            nodal[:, :, :side_nodes].reshape(3, plane_nodes),
            nodal[:, :, 0::side_nodes].reshape(3, plane_nodes),
        ]
    )
    high_layer = jnp.stack(
        [
            nodal[:, side_nodes - 1, :],
            nodal[:, :, plane_nodes - side_nodes :].reshape(3, plane_nodes),
            nodal[:, :, side_nodes - 1 :: side_nodes].reshape(3, plane_nodes),
        ]
    )
    return (low_layer, high_layer)


def cholesky_solve(factor, group_rhs):
    column = group_rhs[:, None]
    middle = lax.linalg.triangular_solve(factor, column, left_side=True, lower=True)
    solved = lax.linalg.triangular_solve(
        factor, middle, left_side=True, lower=True, transpose_a=True
    )
    return solved[:, 0]


def along_sub(faces, offset):
    return shifted(faces, "sub", offset)


def along_grp(faces, offset):
    return shifted(faces, "grp", offset)


def per_device(multipliers, residual, stiff_class, moduli, coarse_panel):
    side_nodes = stiff_class.shape[1]
    plane_nodes = stiff_class.shape[2]
    grid_class = stiff_class[0]
    stiffness = jnp.zeros(grid_class.shape, jnp.float32)
    for level in range(moduli.shape[0]):
        stiffness = stiffness + jnp.where(grid_class == level, moduli[level], 0.0)
    fine_op = build_operator(stiffness, mass_weight, 1.0)
    coarse_op = build_operator(coarsen(stiffness) / 8.0, 8.0 * mass_weight, 4.0)
    corner_ramp = corner_table(side_nodes)
    corner_plane = plane_table(corner_ramp)
    sub_index = lax.axis_index("sub")
    member = lax.axis_index("grp")
    sub_count = lax.axis_size("sub")
    grp_count = lax.axis_size("grp")
    grid_row = sub_index // SPAN
    grid_col = sub_index % SPAN
    upper_ok = jnp.stack(
        [grid_row < sub_count // SPAN - 1, grid_col < SPAN - 1, member < grp_count - 1]
    )
    upper_ok = upper_ok.astype(jnp.float32)[:, None, None]
    lower_ok = jnp.stack([grid_row > 0, grid_col > 0, member > 0])
    lower_ok = lower_ok.astype(jnp.float32)[:, None, None]

    def from_lower(faces):
        moved = jnp.stack(
            [along_sub(faces[0], SPAN), along_sub(faces[1], 1), along_grp(faces[2], 1)]
        )
        return moved * lower_ok

    def from_upper(faces):
        moved = jnp.stack(
            [along_sub(faces[0], -SPAN), along_sub(faces[1], -1), along_grp(faces[2], -1)]
        )
        return moved * upper_ok

    group_matrix = lax.all_gather(coarse_panel[0], "grp", axis=0, tiled=True)
    factor = jnp.linalg.cholesky(group_matrix)
    dual_values = multipliers.reshape(3, 3, plane_nodes) * upper_ok
    misfit = residual.reshape(3, 3, plane_nodes) * upper_ok
    inner_old = jnp.float32(1.0)
    step_size = jnp.float32(1.0)
    direction = misfit
    applied = misfit
    for step_index in range(ITERS):
        precondition_source = spread_faces(misfit, from_lower(misfit))
        precondition_low_layer, precondition_high_layer = face_layers(
            apply_operator(fine_op, precondition_source)
        )
        smoothed = 0.25 * (precondition_high_layer - from_upper(precondition_low_layer)) * upper_ok
        smoothed_low = None
        smoothed, smoothed_low = (smoothed, smoothed_low)
        precond_inner = lax.psum(jnp.sum(misfit * smoothed), ("sub", "grp"))
        if step_index == 0:
            direction = smoothed
        else:
            ratio = precond_inner / inner_old
            direction = smoothed + ratio * direction
        dual_direction_low = from_lower(direction)
        source = spread_faces(direction, dual_direction_low)
        smooth = vcycle(fine_op, coarse_op, source)
        group_rhs = lax.all_gather(
            corner_sums(source, corner_ramp, corner_plane), "grp", axis=0, tiled=True
        )
        solved = cholesky_solve(factor, group_rhs)
        own_values = lax.dynamic_slice_in_dim(solved, member * CORNER_DOFS, CORNER_DOFS)
        low_layer, high_layer = face_layers(
            smooth + corner_spread(own_values, corner_ramp, corner_plane)
        )
        applied = (high_layer - from_upper(low_layer)) * upper_ok
        curve_inner = lax.psum(jnp.sum(direction * applied), ("sub", "grp"))
        step_size = precond_inner / curve_inner
        dual_values = dual_values + step_size * direction
        misfit = misfit - step_size * applied
        inner_old = precond_inner
    shape_out = (1, 9, plane_nodes)
    return (dual_values.reshape(shape_out), misfit.reshape(shape_out))


def solution(mesh):
    return jax.shard_map(
        per_device,
        mesh=mesh,
        in_specs=(
            P(("sub", "grp"), None, None),
            P(("sub", "grp"), None, None),
            P(("sub", "grp"), None, None),
            P(),
            P(("sub", "grp"), None, None),
        ),
        out_specs=(P(("sub", "grp"), None, None), P(("sub", "grp"), None, None)),
        check_vma=False,
    )
```

profile of v0, /device:TPU:1, one launch (start us, length us, event | category | flops | bytes accessed | tf_op | source)
XLA Modules:
  0.0 499.2 jit_solution(12778537057474355719)
XLA Ops:
  1.6 4.9 collective-permute-start.1
  6.5 3.1 collective-permute-start.2
  9.6 4.9 collective-permute-start
  14.7 1.6 fusion.112
  16.4 5.9 %multiply_bitcast_fusion = (f32[16,256]{1,0:T(8,128)S(1)}, f32[1,16,256]{2,1,0:T(8,128)S(1)}) fusion(f32[]{:T(128)} %bitcast.10, s32[1,16,256]{2,1,0:T(8,128)} %param.11, f32[]{:T(128)} %bitcast.9, f32[]{:T(128)} %bitcast.8, f32[]{:T(128)} %bitcast.7, f32[]{:T(128)} %bitcast.6, f32[]{:T(128)} %bitcast.5, f32[]{:T(128)} %bitcast.4, f32[]{:T(128)} %bitcast.3), kind=kLoop, calls=%fused_computation.155 | loop fusion | flops 98304 | bytes 49184 | tf_op jit(solution)/shard_map/mul | solution.py:49
  22.2 1.0 reshape.888
  23.7 9.3 %all-gather = f32[1,96,96]{2,0,1:T(1,128)S(1)} all-gather(f32[1,24,96]{2,0,1:T(1,128)} %bitcast.237), channel_id=2, replica_groups=mesh['sub'=128,'grp'=4] {'grp'}, dimensions={1}, use_global_device_ids=true | all-gather | bytes 46080 | tf_op jit(solution)/shard_map/all_gather | solution.py:230
  33.1 8.8 %cholesky.18 = f32[96,96]{1,0:T(8,128)S(1)} custom-call(f32[96,96]{1,0:T(8,128)S(1)} %fusion.49), custom_call_target="Cholesky" | custom-call | tf_op jit(solution)/shard_map/jit(cholesky)/cholesky | solution.py:231
  46.0 1.3 collective-permute-start.3
  47.5 3.8 collective-permute-start.4
  51.3 1.3 collective-permute-start.5
  53.2 0.9 collective-permute-done.4
  54.1 1.7 collective-permute-done.5
  55.9 4.5 collective-permute-start.7
  60.4 1.9 collective-permute-start.8
  62.2 6.9 %collective-permute-start.6 = (f32[3,256]{1,0:T(4,128)S(1)}, f32[3,256]{1,0:T(4,128)S(1)}, u32[]{:S(2)}, u32[]{:S(2)}) collective-permute-start(f32[3,256]{1,0:T(4,128)S(1)} %get-tuple-element.65), channel_id=1, source_target_pairs={{0,16},{4,20},{8,24},{12,28},{16,32},{20,36},{24,40},{28,44},{32,4... | collective-permute-start | bytes 9224 | tf_op jit(solution)/shard_map/ppermute | solution.py:20
  70.7 7.4 %custom-call.12 = f32[1,96,96]{1,2,0:T(8,128)S(1)} custom-call(f32[1,96,96]{2,1,0:T(8,128)S(1)} %fusion.48), custom_call_target="InvertDiagBlocksLowerTriangular" | custom-call | tf_op jit(solution)/shard_map/triangular_solve/custom-call.2 | solution.py:180
  78.1 1.3 dynamic-slice.2
  84.7 3.2 reshape.856
  89.4 2.1 reshape.858
  93.5 6.9 %all-reduce.108 = f32[96]{0:T(128)S(1)} all-reduce(f32[96]{0:T(128)S(1)} %dynamic-update-slice.3), channel_id=1, replica_groups=mesh['sub'=128,'grp'=4] {'grp'}, use_global_device_ids=true, to_apply=%add.108 | all-reduce | flops 96 | bytes 768 | tf_op jit(solution)/shard_map/triangular_solve/reshape.51 | solution.py:179
  102.4 1.3 collective-permute-start.9
  103.8 1.3 collective-permute-start.11
  105.2 3.0 collective-permute-start.10
  108.2 1.4 fusion.66
  109.9 1.1 collective-permute-done.10
  110.9 1.3 pad_maximum_fusion.3
  112.2 110.4 %all-reduce.110 = (f32[]{:T(128)}, f32[]{:T(128)}) all-reduce(f32[]{:T(128)} %fusion.66, f32[]{:T(128)} %get-tuple-element.48), channel_id=1, replica_groups=mesh['sub'=128,'grp'=4] {'sub','grp'}, use_global_device_ids=true, to_apply=%region_1.2 | all-reduce | flops 2 | bytes 16 | tf_op jit(solution)/shard_map/psum | solution.py:246
  224.7 2.8 collective-permute-start.13
  227.5 1.9 collective-permute-start.14
  229.4 2.4 collective-permute-start.12
  234.6 1.3 collective-permute-start.15
  236.2 2.2 collective-permute-start.16
  238.4 1.3 collective-permute-start.17
  239.9 1.3 collective-permute-done.16
  241.2 1.7 collective-permute-done.17
  243.6 107.0 %psum.30 = f32[]{:T(128)} all-reduce(f32[]{:T(128)} %multiply_reduce_fusion), channel_id=1, replica_groups=mesh['sub'=128,'grp'=4] {'sub','grp'}, use_global_device_ids=true, to_apply=%region_9.12 | all-reduce | flops 1 | bytes 8 | tf_op jit(solution)/shard_map/psum | solution.py:246
  352.1 3.1 collective-permute-start.19
  355.2 1.8 collective-permute-start.20
  356.9 2.8 collective-permute-start.18
  363.3 3.2 reshape.865
  368.0 2.1 reshape.867
  371.4 6.5 %all-reduce.109 = f32[96]{0:T(128)S(1)} all-reduce(f32[96]{0:T(128)S(1)} %dynamic-update-slice.4), channel_id=1, replica_groups=mesh['sub'=128,'grp'=4] {'grp'}, use_global_device_ids=true, to_apply=%add.109 | all-reduce | flops 96 | bytes 768 | tf_op jit(solution)/shard_map/triangular_solve/reshape.51 | solution.py:179
  380.0 1.3 collective-permute-start.21
  381.4 1.3 collective-permute-start.23
  382.7 3.9 collective-permute-start.22
  387.1 1.7 collective-permute-done.22
  389.5 107.0 %psum.31 = f32[]{:T(128)} all-reduce(f32[]{:T(128)} %get-tuple-element.37), channel_id=1, replica_groups=mesh['sub'=128,'grp'=4] {'sub','grp'}, use_global_device_ids=true, to_apply=%region_12.15 | all-reduce | flops 1 | bytes 8 | tf_op jit(solution)/shard_map/psum | solution.py:264
  (399 shorter events, 33.3 us)
Async XLA Ops:
  1.6 42.7 %collective-permute-start.1 = (f32[3,256]{1,0:T(4,128)S(1)}, f32[3,256]{1,0:T(4,128)S(1)}, u32[]{:S(2)}, u32[]{:S(2)}) collective-permute-start(f32[3,256]{1,0:T(4,128)S(1)} %get-tuple-element.73), channel_id=1, source_target_pairs={{0,4},{4,8},{8,12},{12,16},{16,20},{20,24},{24,28},{28,32},{32,36}... | collective-permute-start | bytes 9224 | tf_op jit(solution)/shard_map/ppermute | solution.py:20
  6.5 37.8 %collective-permute-start.2 = (f32[3,256]{1,0:T(4,128)S(1)}, f32[3,256]{1,0:T(4,128)S(1)}, u32[]{:S(2)}, u32[]{:S(2)}) collective-permute-start(f32[3,256]{1,0:T(4,128)S(1)} %get-tuple-element.74), channel_id=1, source_target_pairs={{0,1},{1,2},{2,3},{4,5},{5,6},{6,7},{8,9},{9,10},{10,11},{12,13},{... | collective-permute-start | bytes 9224 | tf_op jit(solution)/shard_map/ppermute | solution.py:20
  9.6 34.7 %collective-permute-start = (f32[3,256]{1,0:T(4,128)S(1)}, f32[3,256]{1,0:T(4,128)S(1)}, u32[]{:S(2)}, u32[]{:S(2)}) collective-permute-start(f32[3,256]{1,0:T(4,128)S(1)} %get-tuple-element.76), channel_id=1, source_target_pairs={{0,16},{4,20},{8,24},{12,28},{16,32},{20,36},{24,40},{28,44},{32,4... | collective-permute-start | bytes 9224 | tf_op jit(solution)/shard_map/ppermute | solution.py:20
  46.0 7.2 %collective-permute-start.3 = (f32[3,256]{1,0:T(4,128)S(1)}, f32[3,256]{1,0:T(4,128)S(1)}, u32[]{:S(2)}, u32[]{:S(2)}) collective-permute-start(f32[3,256]{1,0:T(4,128)S(1)} %get-tuple-element.26), channel_id=1, source_target_pairs={{16,0},{20,4},{24,8},{28,12},{32,16},{36,20},{40,24},{44,28},{48,3... | collective-permute-start | bytes 9224 | tf_op jit(solution)/shard_map/ppermute | solution.py:20
  47.5 6.6 %collective-permute-start.4 = (f32[3,256]{1,0:T(4,128)S(1)}, f32[3,256]{1,0:T(4,128)S(1)}, u32[]{:S(2)}, u32[]{:S(2)}) collective-permute-start(f32[3,256]{1,0:T(4,128)S(1)} %squeeze_stack_reshape.24), channel_id=1, source_target_pairs={{4,0},{8,4},{12,8},{16,12},{20,16},{24,20},{28,24},{32,28},{36,32}... | collective-permute-start | bytes 9224 | tf_op jit(solution)/shard_map/ppermute | solution.py:20
  51.3 4.5 collective-permute-start.5
  55.9 26.1 %collective-permute-start.7 = (f32[3,256]{1,0:T(4,128)S(1)}, f32[3,256]{1,0:T(4,128)S(1)}, u32[]{:S(2)}, u32[]{:S(2)}) collective-permute-start(f32[3,256]{1,0:T(4,128)S(1)} %get-tuple-element.62), channel_id=1, source_target_pairs={{0,4},{4,8},{8,12},{12,16},{16,20},{20,24},{24,28},{28,32},{32,36}... | collective-permute-start | bytes 9224 | tf_op jit(solution)/shard_map/ppermute | solution.py:20
  60.4 21.6 %collective-permute-start.8 = (f32[3,256]{1,0:T(4,128)S(1)}, f32[3,256]{1,0:T(4,128)S(1)}, u32[]{:S(2)}, u32[]{:S(2)}) collective-permute-start(f32[3,256]{1,0:T(4,128)S(1)} %get-tuple-element.63), channel_id=1, source_target_pairs={{0,1},{1,2},{2,3},{4,5},{5,6},{6,7},{8,9},{9,10},{10,11},{12,13},{... | collective-permute-start | bytes 9224 | tf_op jit(solution)/shard_map/ppermute | solution.py:20
  62.2 19.8 %collective-permute-start.6 = (f32[3,256]{1,0:T(4,128)S(1)}, f32[3,256]{1,0:T(4,128)S(1)}, u32[]{:S(2)}, u32[]{:S(2)}) collective-permute-start(f32[3,256]{1,0:T(4,128)S(1)} %get-tuple-element.65), channel_id=1, source_target_pairs={{0,16},{4,20},{8,24},{12,28},{16,32},{20,36},{24,40},{28,44},{32,4... | collective-permute-start | bytes 9224 | tf_op jit(solution)/shard_map/ppermute | solution.py:20
  89.4 134.6 %copy-start.14 = (f32[3,3,256]{2,1,0:T(4,128)S(1)}, f32[3,3,256]{2,1,0:T(4,128)}, u32[]{:S(2)}) copy-start(f32[3,3,256]{2,1,0:T(4,128)} %copy-done.13) | copy-start | bytes 27652
  91.6 141.1 %copy-start.32 = (f32[3]{0:T(128)S(1)}, f32[3]{0:T(128)}, u32[]{:S(2)}) copy-start(f32[3]{0:T(128)} %copy-done.31) | copy-start | bytes 40
  91.6 141.8 %copy-start.35 = (pred[16]{0:T(512)(128)(4,1)S(1)}, pred[16]{0:T(512)(128)(4,1)}, u32[]{:S(2)}) copy-start(pred[16]{0:T(512)(128)(4,1)} %copy-done.34) | copy-start | bytes 52
  91.7 141.8 %copy-start.37 = (pred[16]{0:T(512)(128)(4,1)S(1)}, pred[16]{0:T(512)(128)(4,1)}, u32[]{:S(2)}) copy-start(pred[16]{0:T(512)(128)(4,1)} %copy-done.36) | copy-start | bytes 52
  91.7 141.8 %copy-start.39 = (pred[256]{0:T(512)(128)(4,1)S(1)}, pred[256]{0:T(512)(128)(4,1)}, u32[]{:S(2)}) copy-start(pred[256]{0:T(512)(128)(4,1)} %copy-done.38) | copy-start | bytes 772
  91.7 141.8 %copy-start.41 = (pred[256]{0:T(512)(128)(4,1)S(1)}, pred[256]{0:T(512)(128)(4,1)}, u32[]{:S(2)}) copy-start(pred[256]{0:T(512)(128)(4,1)} %copy-done.40) | copy-start | bytes 772
  91.7 141.8 %copy-start.43 = (pred[256]{0:T(512)(128)(4,1)S(1)}, pred[256]{0:T(512)(128)(4,1)}, u32[]{:S(2)}) copy-start(pred[256]{0:T(512)(128)(4,1)} %copy-done.42) | copy-start | bytes 772
  91.7 141.8 %copy-start.45 = (pred[256]{0:T(512)(128)(4,1)S(1)}, pred[256]{0:T(512)(128)(4,1)}, u32[]{:S(2)}) copy-start(pred[256]{0:T(512)(128)(4,1)} %copy-done.44) | copy-start | bytes 772
  101.2 141.7 %copy-start.49 = (f32[9]{0:T(128)S(1)}, f32[9]{0:T(128)}, u32[]{:S(2)}) copy-start(f32[9]{0:T(128)} %mul.869) | copy-start | bytes 112
  101.2 141.7 %copy-start.51 = (f32[9]{0:T(128)S(1)}, f32[9]{0:T(128)}, u32[]{:S(2)}) copy-start(f32[9]{0:T(128)} %mul.840) | copy-start | bytes 112
  102.1 249.8 %copy-start.29 = (f32[3]{0:T(128)S(1)}, f32[3]{0:T(128)}, u32[]{:S(2)}) copy-start(f32[3]{0:T(128)} %copy-done.28) | copy-start | bytes 40
  102.1 249.8 %copy-start.47 = (f32[3]{0:T(128)S(1)}, f32[3]{0:T(128)}, u32[]{:S(2)}) copy-start(f32[3]{0:T(128)} %copy-done.46) | copy-start | bytes 40
  102.4 7.5 %collective-permute-start.9 = (f32[3,256]{1,0:T(4,128)S(1)}, f32[3,256]{1,0:T(4,128)S(1)}, u32[]{:S(2)}, u32[]{:S(2)}) collective-permute-start(f32[3,256]{1,0:T(4,128)S(1)} %bitcast.253), channel_id=1, source_target_pairs={{16,0},{20,4},{24,8},{28,12},{32,16},{36,20},{40,24},{44,28},{48,3... | collective-permute-start | bytes 9224 | tf_op jit(solution)/shard_map/ppermute | solution.py:20
  103.8 6.1 %collective-permute-start.11 = (f32[3,256]{1,0:T(4,128)S(1)}, f32[3,256]{1,0:T(4,128)S(1)}, u32[]{:S(2)}, u32[]{:S(2)}) collective-permute-start(f32[3,256]{1,0:T(4,128)S(1)} %squeeze_stack_reshape.27), channel_id=1, source_target_pairs={{1,0},{2,1},{3,2},{5,4},{6,5},{7,6},{9,8},{10,9},{11,10},{13,12},{... | collective-permute-start | bytes 9224 | tf_op jit(solution)/shard_map/ppermute | solution.py:20
  105.2 5.8 %collective-permute-start.10 = (f32[3,256]{1,0:T(4,128)S(1)}, f32[3,256]{1,0:T(4,128)S(1)}, u32[]{:S(2)}, u32[]{:S(2)}) collective-permute-start(f32[3,256]{1,0:T(4,128)S(1)} %squeeze_stack_reshape.26), channel_id=1, source_target_pairs={{4,0},{8,4},{12,8},{16,12},{20,16},{24,20},{28,24},{32,28},{36,32}... | collective-permute-start | bytes 9224 | tf_op jit(solution)/shard_map/ppermute | solution.py:20
  224.7 7.9 %collective-permute-start.13 = (f32[3,256]{1,0:T(4,128)S(1)}, f32[3,256]{1,0:T(4,128)S(1)}, u32[]{:S(2)}, u32[]{:S(2)}) collective-permute-start(f32[3,256]{1,0:T(4,128)S(1)} %get-tuple-element.54), channel_id=1, source_target_pairs={{0,4},{4,8},{8,12},{12,16},{16,20},{20,24},{24,28},{28,32},{32,36}... | collective-permute-start | bytes 9224 | tf_op jit(solution)/shard_map/ppermute | solution.py:20
  227.5 5.1 %collective-permute-start.14 = (f32[3,256]{1,0:T(4,128)S(1)}, f32[3,256]{1,0:T(4,128)S(1)}, u32[]{:S(2)}, u32[]{:S(2)}) collective-permute-start(f32[3,256]{1,0:T(4,128)S(1)} %get-tuple-element.55), channel_id=1, source_target_pairs={{0,1},{1,2},{2,3},{4,5},{5,6},{6,7},{8,9},{9,10},{10,11},{12,13},{... | collective-permute-start | bytes 9224 | tf_op jit(solution)/shard_map/ppermute | solution.py:20
  229.4 3.2 collective-permute-start.12
  231.8 128.5 %copy-start.1 = (f32[1,9,256]{2,1,0:T(8,128)}, f32[1,9,256]{2,1,0:T(8,128)S(1)}, u32[]{:S(2)}) copy-start(f32[1,9,256]{2,1,0:T(8,128)S(1)} %stack.183) | copy-start | bytes 27652
  231.8 128.5 %copy-start.3 = (f32[1,9,256]{2,1,0:T(8,128)}, f32[1,9,256]{2,1,0:T(8,128)S(1)}, u32[]{:S(2)}) copy-start(f32[1,9,256]{2,1,0:T(8,128)S(1)} %stack.182) | copy-start | bytes 27652
  233.7 128.2 %copy-start.54 = (f32[1,16]{1,0:T(1,128)S(1)}, f32[1,16]{1,0:T(1,128)}, u32[]{:S(2)}) copy-start(f32[1,16]{1,0:T(1,128)} %copy-done.53) | copy-start | bytes 196
  233.7 128.2 %copy-start.56 = (f32[1,16]{1,0:T(1,128)S(1)}, f32[1,16]{1,0:T(1,128)}, u32[]{:S(2)}) copy-start(f32[1,16]{1,0:T(1,128)} %copy-done.55) | copy-start | bytes 196
  234.6 5.3 %collective-permute-start.15 = (f32[3,256]{1,0:T(4,128)S(1)}, f32[3,256]{1,0:T(4,128)S(1)}, u32[]{:S(2)}, u32[]{:S(2)}) collective-permute-start(f32[3,256]{1,0:T(4,128)S(1)} %get-tuple-element.22), channel_id=1, source_target_pairs={{16,0},{20,4},{24,8},{28,12},{32,16},{36,20},{40,24},{44,28},{48,3... | collective-permute-start | bytes 9224 | tf_op jit(solution)/shard_map/ppermute | solution.py:20
  236.2 5.0 %collective-permute-start.16 = (f32[3,256]{1,0:T(4,128)S(1)}, f32[3,256]{1,0:T(4,128)S(1)}, u32[]{:S(2)}, u32[]{:S(2)}) collective-permute-start(f32[3,256]{1,0:T(4,128)S(1)} %squeeze_stack_reshape.28), channel_id=1, source_target_pairs={{4,0},{8,4},{12,8},{16,12},{20,16},{24,20},{28,24},{32,28},{36,32}... | collective-permute-start | bytes 9224 | tf_op jit(solution)/shard_map/ppermute | solution.py:20
  238.4 4.5 collective-permute-start.17
  352.1 8.5 %collective-permute-start.19 = (f32[3,256]{1,0:T(4,128)S(1)}, f32[3,256]{1,0:T(4,128)S(1)}, u32[]{:S(2)}, u32[]{:S(2)}) collective-permute-start(f32[3,256]{1,0:T(4,128)S(1)} %get-tuple-element.43), channel_id=1, source_target_pairs={{0,4},{4,8},{8,12},{12,16},{16,20},{20,24},{24,28},{28,32},{32,36}... | collective-permute-start | bytes 9224 | tf_op jit(solution)/shard_map/ppermute | solution.py:20
  355.2 5.4 %collective-permute-start.20 = (f32[3,256]{1,0:T(4,128)S(1)}, f32[3,256]{1,0:T(4,128)S(1)}, u32[]{:S(2)}, u32[]{:S(2)}) collective-permute-start(f32[3,256]{1,0:T(4,128)S(1)} %get-tuple-element.44), channel_id=1, source_target_pairs={{0,1},{1,2},{2,3},{4,5},{5,6},{6,7},{8,9},{9,10},{10,11},{12,13},{... | collective-permute-start | bytes 9224 | tf_op jit(solution)/shard_map/ppermute | solution.py:20
  356.9 3.7 collective-permute-start.18
  368.0 129.8 %copy-start.2 = (f32[1,9,256]{2,1,0:T(8,128)S(1)}, f32[1,9,256]{2,1,0:T(8,128)}, u32[]{:S(2)}) copy-start(f32[1,9,256]{2,1,0:T(8,128)} %copy-done.1) | copy-start | bytes 27652
  368.0 129.8 %copy-start.4 = (f32[1,9,256]{2,1,0:T(8,128)S(1)}, f32[1,9,256]{2,1,0:T(8,128)}, u32[]{:S(2)}) copy-start(f32[1,9,256]{2,1,0:T(8,128)} %copy-done.3) | copy-start | bytes 27652
  368.0 129.8 %copy-start.6 = (f32[1,9,256]{2,1,0:T(8,128)S(1)}, f32[1,9,256]{2,1,0:T(8,128)}, u32[]{:S(2)}) copy-start(f32[1,9,256]{2,1,0:T(8,128)} %copy-done.5) | copy-start | bytes 27652
  370.2 127.7 %copy-start.8 = (f32[1,9,256]{2,1,0:T(8,128)S(1)}, f32[1,9,256]{2,1,0:T(8,128)}, u32[]{:S(2)}) copy-start(f32[1,9,256]{2,1,0:T(8,128)} %copy-done.7) | copy-start | bytes 27652
  370.2 127.7 %copy-start.10 = (f32[1,9,256]{2,1,0:T(8,128)S(1)}, f32[1,9,256]{2,1,0:T(8,128)}, u32[]{:S(2)}) copy-start(f32[1,9,256]{2,1,0:T(8,128)} %stack.166) | copy-start | bytes 27652
  370.2 127.7 %copy-start.12 = (f32[1,9,256]{2,1,0:T(8,128)S(1)}, f32[1,9,256]{2,1,0:T(8,128)}, u32[]{:S(2)}) copy-start(f32[1,9,256]{2,1,0:T(8,128)} %stack.171) | copy-start | bytes 27652
  370.2 127.7 %copy-start.33 = (f32[1,9,256]{2,0,1:T(1,128)S(1)}, f32[1,9,256]{2,0,1:T(1,128)}, u32[]{:S(2)}) copy-start(f32[1,9,256]{2,0,1:T(1,128)} %param.9) | copy-start | bytes 27652
  370.2 127.7 %copy-start.50 = (f32[9]{0:T(128)S(1)}, f32[9]{0:T(128)}, u32[]{:S(2)}) copy-start(f32[9]{0:T(128)} %mul.869) | copy-start | bytes 112
  380.0 7.1 %collective-permute-start.21 = (f32[3,256]{1,0:T(4,128)S(1)}, f32[3,256]{1,0:T(4,128)S(1)}, u32[]{:S(2)}, u32[]{:S(2)}) collective-permute-start(f32[3,256]{1,0:T(4,128)S(1)} %get-tuple-element.19), channel_id=1, source_target_pairs={{16,0},{20,4},{24,8},{28,12},{32,16},{36,20},{40,24},{44,28},{48,3... | collective-permute-start | bytes 9224 | tf_op jit(solution)/shard_map/ppermute | solution.py:20
  381.4 5.7 %collective-permute-start.23 = (f32[3,256]{1,0:T(4,128)S(1)}, f32[3,256]{1,0:T(4,128)S(1)}, u32[]{:S(2)}, u32[]{:S(2)}) collective-permute-start(f32[3,256]{1,0:T(4,128)S(1)} %squeeze_stack_reshape.31), channel_id=1, source_target_pairs={{1,0},{2,1},{3,2},{5,4},{6,5},{7,6},{9,8},{10,9},{11,10},{13,12},{... | collective-permute-start | bytes 9224 | tf_op jit(solution)/shard_map/ppermute | solution.py:20
  382.7 6.0 %collective-permute-start.22 = (f32[3,256]{1,0:T(4,128)S(1)}, f32[3,256]{1,0:T(4,128)S(1)}, u32[]{:S(2)}, u32[]{:S(2)}) collective-permute-start(f32[3,256]{1,0:T(4,128)S(1)} %squeeze_stack_reshape.30), channel_id=1, source_target_pairs={{4,0},{8,4},{12,8},{16,12},{20,16},{24,20},{28,24},{32,28},{36,32}... | collective-permute-start | bytes 9224 | tf_op jit(solution)/shard_map/ppermute | solution.py:20
  (33 other events, 2023.0 us)
where the time goes:
time: 501 us; the launch traced here: 499 us
  blocking collectives  347 us (69%)
  starting transfers between devices  64.1 us (13%)
  other arithmetic  36.9 us (7%)
  local copies, waits for them, and re-layouts  30.1 us (6%)
  waiting for transfers between devices  8.44 us (2%)
  between operations  7.3 us (1%)
  matrix products  5.27 us (1%)
    psum x2, blocking collectives, per_device(): precond_inner = lax.psum(jnp.sum(misfit * smoothed), ('sub', 'grp'))  217 us
    psum x1, blocking collectives, per_device(): curve_inner = lax.psum(jnp.sum(direction * applied), ('sub', 'grp'))  107 us
    ppermute x24, starting transfers between devices, shifted(): return lax.ppermute(block, axis, route)  64.1 us
    another operation x2, blocking collectives, cholesky_solve(): lax.linalg.triangular_solve(factor, column, left_side=True, lower=True)  13.4 us
  transfers between devices with their start and end apart: 24, of which 7 were waited for; matrix products, arithmetic and copies ran while one was open for 7% of the time, Pallas kernels for 0%

commit v1 on v0

v1 whole, which is shorter than its diff:
```python
import functools

import jax
import jax.numpy as jnp
from jax import lax
from jax.experimental import pallas as pl
from jax.experimental.pallas import tpu as pltpu
from jax.sharding import PartitionSpec as P

MESH = pl.DeviceIdType.MESH
F32 = jnp.float32
SPAN = 4
CORNER = 24
DAMP = 0.8
HI = lax.Precision.HIGHEST


def roll(x, shift, axis):
    shift = shift % x.shape[axis]
    return x if shift == 0 else pltpu.roll(x, shift, axis)


def iota(shape, axis):
    return lax.broadcasted_iota(jnp.int32, shape, axis)


def m3(coef, field):
    return (field.reshape(3, 16, 256) * coef[None]).reshape(48, 256)


def neighbours(v, k):
    return (
        roll(v, -k, 0),
        roll(v, k, 0),
        roll(v, -16 * k, 1),
        roll(v, 16 * k, 1),
        roll(v, -k, 1),
        roll(v, k, 1),
    )


def weighted(coefs, v, k):
    terms = [m3(a, n) for a, n in zip(coefs, neighbours(v, k))]
    return (terms[0] + terms[1]) + (terms[2] + terms[3]) + (terms[4] + terms[5])


def pair_sum(v):
    rows, lanes = iota(v.shape, 0), iota(v.shape, 1)
    v = v + jnp.where(rows % 2 == 0, roll(v, -1, 0), roll(v, 1, 0))
    v = v + jnp.where(lanes % 32 < 16, roll(v, -16, 1), roll(v, 16, 1))
    return v + jnp.where(lanes % 2 == 0, roll(v, -1, 1), roll(v, 1, 1))


def edge_weights(s, k, scale):
    rows, lanes = iota(s.shape, 0), iota(s.shape, 1)
    coordinate = (rows, lanes // 16, lanes % 16)
    shifts = ((k, 0), (16 * k, 1), (k, 1))
    weights = []
    for where, (step, axis) in zip(coordinate, shifts):
        up = jnp.where(where < 16 - k, scale * (s + roll(s, -step, axis)), 0.0)
        low = jnp.where(where >= k, scale * (s + roll(s, step, axis)), 0.0)
        weights += [up, low]
    return weights, sum(weights[1:], weights[0])


def place(own, low):
    lane = iota((16, 128), 1)
    row = iota((16, 128), 0)
    inner = lane % 16
    parts = []
    for c in range(3):
        halves = []
        for h in range(2):
            r = 3 * h + c
            t = jnp.where(row == 15, own[r : r + 1, :], 0.0)
            t = t - jnp.where(row == 0, low[r : r + 1, :], 0.0)
            if h == 1:
                t = t + jnp.where(lane >= 112, roll(own[8:24], -16 - 16 * c, 1), 0.0)
            else:
                t = t - jnp.where(lane < 16, roll(low[8:24], -16 * c, 1), 0.0)
            t = t + jnp.where(inner == 15, roll(own[24:40], 15 - c - 3 * h, 1), 0.0)
            t = t - jnp.where(inner == 0, roll(low[24:40], -c - 3 * h, 1), 0.0)
            halves.append(t)
        parts.append(jnp.concatenate(halves, axis=1))
    return jnp.concatenate(parts, axis=0)


def pack(v, buf, high):
    lane = iota((16, 128), 1)
    inner = lane % 16
    at = 15 if high else 0
    y = z = None
    for c in range(3):
        for h in range(2):
            r = 3 * h + c
            part = v[16 * c : 16 * c + 16, 128 * h : 128 * h + 128]
            buf[r : r + 1, :] = part[at : at + 1, :]
            t = roll(jnp.where(inner == at, part, 0.0), c + 3 * h - at, 1)
            z = t if z is None else z + t
        if high:
            part = v[16 * c : 16 * c + 16, 128:256]
            t = roll(jnp.where(lane >= 112, part, 0.0), 16 + 16 * c, 1)
        else:
            part = v[16 * c : 16 * c + 16, 0:128]
            t = roll(jnp.where(lane < 16, part, 0.0), 16 * c, 1)
        y = t if y is None else y + t
    buf[6:8, :] = jnp.zeros((2, 128), F32)
    buf[8:24, :] = y
    buf[24:40, :] = z


def from_rows(rows, buf):
    lane = iota((16, 256), 1)
    row = iota((16, 256), 0)
    m, n = iota((256, 128), 0) % 16, iota((256, 128), 1)
    to_y = jnp.where(m == n % 16, 1.0, 0.0)
    to_z = jnp.where(n == (m % 8) * 16 + 3 * (m // 8), 1.0, 0.0)

    def spread(first):
        return jnp.concatenate(
            [jnp.where(lane // 16 == row, rows[first + c : first + c + 1, :], 0.0) for c in range(3)],
            axis=0,
        )

    y = jnp.dot(spread(3), to_y, precision=HI, preferred_element_type=F32)
    z = jnp.dot(spread(6), to_z, precision=HI, preferred_element_type=F32)
    group = iota((16, 128), 1) // 16
    buf[0:3, :] = rows[0:3, 0:128]
    buf[3:6, :] = rows[0:3, 128:256]
    buf[6:8, :] = jnp.zeros((2, 128), F32)
    buf[8:24, :] = sum(jnp.where(group == c, y[16 * c : 16 * c + 16], 0.0) for c in range(3))
    buf[24:40, :] = sum(roll(z[16 * c : 16 * c + 16], c, 1) for c in range(3))


def to_rows(faces, buf, slot):
    lane = iota((16, 256), 1)
    row = iota((16, 256), 0)
    n, m = iota((128, 256), 0), iota((128, 256), 1) % 16
    from_y = jnp.where(n == m, 1.0, 0.0)
    from_z = jnp.where(n == (m % 8) * 16 + 3 * (m // 8), 1.0, 0.0)
    y = jnp.concatenate([roll(faces[8:24], -16 * c, 1) for c in range(3)], axis=0)
    z = jnp.concatenate([roll(faces[24:40], -c, 1) for c in range(3)], axis=0)
    y = jnp.dot(y, from_y, precision=HI, preferred_element_type=F32)
    z = jnp.dot(z, from_z, precision=HI, preferred_element_type=F32)
    buf[slot, 0:3, 0:128] = faces[0:3]
    buf[slot, 0:3, 128:256] = faces[3:6]
    for c in range(3):
        for first, t in ((3, y), (6, z)):
            t = jnp.where(lane // 16 == row, t[16 * c : 16 * c + 16], 0.0)
            buf[slot, first + c : first + c + 1, :] = jnp.sum(t, axis=0, keepdims=True)


def partial_dot(a, b):
    t = jnp.sum(a * b, axis=0, keepdims=True)
    return t[:, 0:128] + t[:, 128:256]


def eliminate(first, last, matrix):
    size = matrix.shape[0]
    row_a, lane_a = iota((size, 128), 0), iota((size, 128), 1)
    row_b, lane_b = iota((8, 128), 0), iota((8, 128), 1)
    lane_w = iota((1, 128), 1)

    def block(k, a):
        matrix[...] = a
        base = pl.multiple_of(k * 8, 8)
        b = matrix[pl.ds(base, 8), :]
        local_a = row_a - base
        for t in range(0, 8, 2):
            r0, r1 = b[t : t + 1, :], b[t + 1 : t + 2, :]
            p, q, s = r0[:, t : t + 1], r0[:, t + 1 : t + 2], r1[:, t + 1 : t + 2]
            inverse = 1.0 / (p * s - q * q)
            p, q, s = p * inverse, q * inverse, s * inverse
            w0, w1 = s * r0 - q * r1, p * r1 - q * r0
            w0 = jnp.where(lane_w == t, s, jnp.where(lane_w == t + 1, -q, w0))
            w1 = jnp.where(lane_w == t, -q, jnp.where(lane_w == t + 1, p, w1))

            def update(x, row, lane):
                rows = x.shape[0]
                column = row[:, 0:1]
                c0 = jnp.where(column == t, -1.0, jnp.where(column == t + 1, 0.0, x[:, t : t + 1]))
                c1 = jnp.where(column == t, 0.0, jnp.where(column == t + 1, -1.0, x[:, t + 1 : t + 2]))
                hit = (row == t) | (row == t + 1) | (lane == t) | (lane == t + 1)
                return jnp.where(hit, 0.0, x) - c0 * w0 - c1 * w1

            a, b = update(a, local_a, lane_a), update(b, row_b, lane_b)
        return roll(a, -8, 1)

    matrix[...] = lax.fori_loop(first, last, block, matrix[...])


def kernel(
    G, Y, Z, mult_ref, res_ref, class_ref, moduli_ref, panel_ref, lam_ref, out_ref,
    matrix, panel, sent_hi, sent_lo, got_hi, got_lo, corner_out, corner_in,
    tiles, x_in, yc_in, z_in, rows, send_sem, recv_sem,
):
    sub, member = lax.axis_index("sub"), lax.axis_index("grp")
    n_sub = Y * Z * 2
    grid_row, grid_col = sub // SPAN, sub % SPAN
    upper = (
        ((sub + SPAN) % n_sub, member),
        (grid_row * SPAN + (grid_col + 1) % SPAN, member),
        (sub, (member + 1) % G),
    )
    lower = (
        ((sub + n_sub - SPAN) % n_sub, member),
        (grid_row * SPAN + (grid_col + SPAN - 1) % SPAN, member),
        (sub, (member + G - 1) % G),
    )
    upper_ok = [
        (grid_row < n_sub // SPAN - 1).astype(F32),
        (grid_col < SPAN - 1).astype(F32),
        (member < G - 1).astype(F32),
    ]
    lower_ok = [
        (grid_row > 0).astype(F32),
        (grid_col > 0).astype(F32),
        (member > 0).astype(F32),
    ]
    core, z, y = sub % 2, (sub // 2) % Z, sub // (2 * Z)
    by_distance = lambda n: sorted(range(1, n), key=lambda i: -min(i, n - i))
    x_partners = [(sub, (member + i) % G) for i in by_distance(G)]
    yc_partners = [
        (((y + i) % Y * Z + z) * 2 + (core + c) % 2, member)
        for i in by_distance(Y) + [0]
        for c in (1, 0)
        if (i, c) != (0, 0)
    ]
    z_partners = [((y * Z + (z + i) % Z) * 2 + core, member) for i in by_distance(Z)]

    barrier = pltpu.get_barrier_semaphore()
    greeted = z_partners + list(upper) + list(lower) + yc_partners + x_partners
    for device in greeted:
        pl.semaphore_signal(barrier, inc=1, device_id=device, device_id_type=MESH)

    copies = []

    def send(src, dst, device):
        i = len(copies)
        copy = pltpu.make_async_remote_copy(
            src_ref=src, dst_ref=dst, send_sem=send_sem.at[i], recv_sem=recv_sem.at[i],
            device_id=device, device_id_type=MESH,
        )
        copy.start()
        copies.append(copy)
        return copy

    def wait(group):
        for copy in group:
            copy.wait_recv()

    spans = ((0, 8), (8, 24), (24, 40))
    order = (0, 2, 1)

    def exchange(e, both=True, up=True):
        group = []
        for k in order:
            first, last = spans[k]
            if up:
                group.append(
                    send(sent_hi.at[e, first:last], got_hi.at[e, first:last], upper[k])
                )
            if both:
                group.append(
                    send(sent_lo.at[e, first:last], got_lo.at[e, first:last], lower[k])
                )
        return group

    face_row = iota((40, 128), 0)

    def face_mask(ok):
        return jnp.where(face_row < 8, ok[0], jnp.where(face_row < 24, ok[1], ok[2]))

    up_mask, low_mask = face_mask(upper_ok), face_mask(lower_ok)
    row9 = iota((9, 256), 0)
    row_mask = jnp.where(
        row9 < 3, upper_ok[0], jnp.where(row9 < 6, upper_ok[1], upper_ok[2])
    )

    size = G * CORNER
    own_rows = pl.ds(pl.multiple_of(member * CORNER, 8), CORNER)
    panel[...] = jnp.zeros((CORNER, 128), F32)
    panel[:, 0:size] = panel_ref[0]
    matrix[own_rows, :] = panel[...]

    residual = res_ref[0] * row_mask
    from_rows(residual, sent_hi.at[0])
    rows[0] = residual

    classes = class_ref[0]
    stiffness = jnp.zeros((16, 256), F32)
    for level in range(8):
        stiffness = stiffness + jnp.where(classes == level, moduli_ref[level], 0.0)
    weight, total = edge_weights(stiffness, 1, 0.5)
    diagonal = 0.5 * stiffness + total
    scale = DAMP / diagonal
    relax = [scale * w for w in weight]
    block_mean = pair_sum(stiffness) * 0.125
    coarse_weight, coarse_total = edge_weights(block_mean, 2, 2.0)
    coarse_scale = DAMP / (4.0 * block_mean + coarse_total)
    coarse_relax = [coarse_scale * w for w in coarse_weight]

    def operator(v):
        return m3(diagonal, v) - weighted(weight, v, 1)

    def vcycle(f):
        g = m3(scale, f)
        v = g
        v = (1.0 - DAMP) * v + g + weighted(relax, v, 1)
        h = m3(coarse_scale, pair_sum(f - operator(v)))
        e = h
        for _ in range(3):
            e = (1.0 - DAMP) * e + h + weighted(coarse_relax, e, 2)
        v = v + e
        for _ in range(2):
            v = (1.0 - DAMP) * v + g + weighted(relax, v, 1)
        return v

    lanes = iota((1, 256), 1)
    ramp_y = (lanes // 16).astype(F32) / 15.0
    ramp_z = (lanes % 16).astype(F32) / 15.0
    plane = [
        by * bz for by in (1.0 - ramp_y, ramp_y) for bz in (1.0 - ramp_z, ramp_z)
    ]
    ramp_x = iota((16, 256), 0).astype(F32) / 15.0
    row8, lane8 = iota((8, 128), 0), iota((8, 128), 1)
    row8w = iota((8, 256), 0)
    plane8 = sum(jnp.where(row8w % 4 == n, plane[n], 0.0) for n in range(4))

    def corner_sums(f):
        t = jnp.zeros((8, 256), F32)
        for c in range(3):
            part = f[16 * c : 16 * c + 16]
            for a, ramp in ((0, 1.0 - ramp_x), (1, ramp_x)):
                line = jnp.sum(part * ramp, axis=0, keepdims=True)
                t = t + jnp.where(row8w == 2 * c + a, line, 0.0)
        result = jnp.zeros((8, 128), F32)
        for n in range(4):
            s = t * plane[n]
            s = jnp.sum(s[:, 0:128] + s[:, 128:256], axis=1, keepdims=True)
            at = (lane8 == member * CORNER + row8 * 4 + n) & (row8 < 6)
            result = result + jnp.where(at, s, 0.0)
        return result

    def corner_send(e, f):
        corner_out[e] = corner_sums(f)
        return [
            send(corner_out.at[e], corner_in.at[e, i], device)
            for i, device in enumerate(x_partners)
        ]

    def corner_field(e):
        rhs = corner_out[e]
        for i in range(G - 1):
            rhs = rhs + corner_in[e, i]
        rhs = jnp.sum(rhs, axis=0, keepdims=True)
        solved = jnp.sum(matrix[own_rows, :] * rhs, axis=1, keepdims=True)
        parts = []
        for c in range(3):
            t = solved[8 * c : 8 * c + 8] * plane8
            t0 = jnp.sum(jnp.where(row8w < 4, t, 0.0), axis=0, keepdims=True)
            t1 = jnp.sum(jnp.where(row8w >= 4, t, 0.0), axis=0, keepdims=True)
            parts.append((1.0 - ramp_x) * t0 + ramp_x * t1)
        return jnp.concatenate(parts, axis=0)

    pl.semaphore_wait(barrier, len(greeted))

    group = exchange(0, both=False)
    panels = [send(panel, matrix.at[own_rows, :], device) for device in x_partners]
    wait(group)
    f_r = place(sent_hi[0], got_hi[0] * low_mask)

    image = operator(f_r)
    pack(image, sent_hi.at[1], True)
    pack(image, sent_lo.at[1], False)
    group = exchange(1)
    dots = [0.25 * partial_dot(f_r, image)]
    wait(panels)
    half = size // 16
    eliminate(0, half, matrix)
    wait(group)
    u = (sent_hi[1] - got_lo[1]) * (0.25 * up_mask)
    f_u = place(u, (got_hi[1] - sent_lo[1]) * (0.25 * low_mask))

    group = corner_send(0, f_u)
    v = vcycle(f_u)
    eliminate(half, 2 * half, matrix)
    matrix[...] = roll(matrix[...], size - 128, 1)
    wait(group)
    v = v + corner_field(0)
    pack(v, sent_hi.at[2], True)
    pack(v, sent_lo.at[2], False)
    group = exchange(2)
    dots.append(partial_dot(f_u, v))
    to_rows(u, rows, 1)
    wait(group)
    q = (sent_hi[2] - got_lo[2]) * up_mask
    f_q = place(q, (got_hi[2] - sent_lo[2]) * low_mask)

    image = operator(f_q)
    pack(image, sent_hi.at[3], True)
    pack(image, sent_lo.at[3], False)
    group = exchange(3)
    dots.append(0.25 * partial_dot(f_r, image))
    dots.append(0.25 * partial_dot(f_q, image))
    to_rows(q, rows, 2)
    wait(group)
    w = (sent_hi[3] - got_lo[3]) * (0.25 * up_mask)
    f_w = place(w, (got_hi[3] - sent_lo[3]) * (0.25 * low_mask))

    group = corner_send(1, f_w)
    v = vcycle(f_w)
    wait(group)
    v = v + corner_field(1)
    dots.append(partial_dot(f_u, v))
    dots.append(partial_dot(f_w, v))

    tile = jnp.zeros((8, 128), F32)
    for i, d in enumerate(dots):
        tile = tile + jnp.where(row8 == i, d, 0.0)

    def spread(slot, landing, partners):
        tiles[slot] = tile
        return [
            send(tiles.at[slot], landing.at[i], device) for i, device in enumerate(partners)
        ]

    def collect(group, landing):
        wait(group)
        total = tile
        for i in range(landing.shape[0]):
            total = total + landing[i]
        return total

    group = spread(0, x_in, x_partners)
    pack(v, sent_hi.at[4], True)
    pack(v, sent_lo.at[4], False)
    last = exchange(4, up=False)
    to_rows(w, rows, 3)
    tile = collect(group, x_in)
    group = spread(1, yc_in, yc_partners)
    wait(last)
    to_rows((sent_hi[4] - got_lo[4]) * up_mask, rows, 4)
    tile = collect(group, yc_in)
    group = spread(2, z_in, z_partners)
    tile = collect(group, z_in)

    sums = jnp.sum(tile, axis=1, keepdims=True)
    ru, uq, rw, qw, us, ws = [sums[i : i + 1, :] for i in range(6)]
    a = ru / uq
    next_inner = ru - a * (rw + uq) + a * a * qw
    c = 1.0 + next_inner / ru
    curve = c * c * uq - c * a * (us + qw) + a * a * ws
    b = next_inner / curve
    first, second = a + b * c, a * b
    lam_ref[0] = mult_ref[0] * row_mask + first * rows[1] - second * rows[3]
    out_ref[0] = rows[0] - first * rows[2] + second * rows[4]
    for copy in copies:
        copy.wait_send()


def solution(mesh):
    G, n_sub = mesh.shape["grp"], mesh.shape["sub"]
    Z = min(16, n_sub // 2)
    Y = n_sub // (2 * Z)
    size = G * CORNER
    copies = 3 + 3 * 6 + 3 + 4 * (G - 1) + (2 * Y - 1) + (Z - 1)

    def per_device(multipliers, residual, stiff_class, moduli, coarse_panel):
        vmem = pl.BlockSpec(memory_space=pltpu.VMEM)
        return pl.pallas_call(
            functools.partial(kernel, G, Y, Z),
            out_shape=[jax.ShapeDtypeStruct((1, 9, 256), F32)] * 2,
            in_specs=[vmem, vmem, vmem, pl.BlockSpec(memory_space=pltpu.SMEM), vmem],
            out_specs=[vmem, vmem],
            scratch_shapes=[
                pltpu.VMEM((size, 128), F32),
                pltpu.VMEM((CORNER, 128), F32),
                pltpu.VMEM((5, 40, 128), F32),
                pltpu.VMEM((5, 40, 128), F32),
                pltpu.VMEM((5, 40, 128), F32),
                pltpu.VMEM((5, 40, 128), F32),
                pltpu.VMEM((2, 8, 128), F32),
                pltpu.VMEM((2, G - 1, 8, 128), F32),
                pltpu.VMEM((3, 8, 128), F32),
                pltpu.VMEM((G - 1, 8, 128), F32),
                pltpu.VMEM((2 * Y - 1, 8, 128), F32),
                pltpu.VMEM((Z - 1, 8, 128), F32),
                pltpu.VMEM((5, 9, 256), F32),
                pltpu.SemaphoreType.DMA((copies,)),
                pltpu.SemaphoreType.DMA((copies,)),
            ],
            compiler_params=pltpu.CompilerParams(
                collective_id=0, has_side_effects=True, vmem_limit_bytes=32 * 1024 * 1024
            ),
            name="feti",
        )(multipliers, residual, stiff_class, moduli, coarse_panel)

    device = P(("sub", "grp"), None, None)
    return jax.shard_map(
        per_device,
        mesh=mesh,
        in_specs=(device, device, device, P(), device),
        out_specs=(device, device),
        check_vma=False,
    )
```

time: 501 us -> 65.8 us (0.13)
  blocking collectives: 347 us -> 0 us
  starting transfers between devices: 64.1 us -> 0 us
  Pallas kernels: 0 us -> 62.2 us
  other arithmetic: 36.9 us -> 0 us
  local copies, waits for them, and re-layouts: 30.1 us -> 2.64 us
  waiting for transfers between devices: 8.44 us -> 0 us
  between operations: 7.3 us -> 0.68 us
  matrix products: 5.27 us -> 0 us
    psum x3 -> x0, blocking collectives: 324 us -> none  [the longest x2 217 us: per_device(): precond_inner = lax.psum(jnp.sum(misfit * smoothed), ('sub', 'grp'))]
    ppermute x24 -> x0, starting transfers between devices: 64.1 us -> none  [shifted(): return lax.ppermute(block, axis, route)]
    pallas_call x0 -> x1, Pallas kernels: none -> 62.2 us  [per_device(): pl.pallas_call(functools.partial(kernel, G, Y, Z), out_shape=[jax.ShapeDt...]
    another operation x10 -> x0, other arithmetic: 19.5 us -> none  [the longest x3 9.45 us: per_device(): factor = jnp.linalg.cholesky(group_matrix)]
    another operation x2 -> x0, blocking collectives: 13.4 us -> none  [cholesky_solve(): lax.linalg.triangular_solve(factor, column, left_side=True, lower=True)]
    reshape x19 -> x0, local copies, waits for them, and re-layouts: 12.7 us -> none  [the longest x2 6.33 us: coarsen(): values.reshape(leading + (half_nodes, 2, half_nodes, 2, half_nodes, 2))]
    mul x62 -> x0, other arithmetic: 9.68 us -> none  [the longest x1 5.85 us: apply_operator(): result = mass_term * nodal]
    all_gather x1 -> x0, blocking collectives: 9.29 us -> none  [per_device(): group_matrix = lax.all_gather(coarse_panel[0], 'grp', axis=0, tiled=True)]
  transfers between devices with their start and end apart: 24 -> 0, of which waited for: 7 -> 0; matrix products, arithmetic and copies ran while one was open for 7% -> 0% of each run, Pallas kernels for 0% -> 0%
where the time goes in v1:
time: 65.8 us; the launch traced here: 65.5 us
  Pallas kernels  62.2 us (95%)
  local copies, waits for them, and re-layouts  2.64 us (4%)
  between operations  0.68 us (1%)
    pallas_call x1, Pallas kernels, per_device(): pl.pallas_call(functools.partial(kernel, G, Y, Z), out_shape=[jax.ShapeDt...  62.2 us
    unnamed x10, local copies, waits for them, and re-layouts  1.42 us

profile of v1, /device:TPU:1, one launch (start us, length us, event | category | flops | bytes accessed | tf_op | source)
XLA Modules:
  0.0 65.5 jit_solution(817593401853844166)
XLA Ops:
  0.6 0.0 copy-start.3
  0.6 0.0 copy-start.1
  0.6 0.7 %copy.7.mult_ref = f32[1,9,256]{2,1,0:T(8,128)S(1)} copy(f32[1,9,256]{2,0,1:T(1,128)} %param.5) | data formatting | bytes 18432 | tf_op args[0]
  1.4 0.0 copy-done.3
  1.4 0.0 copy-start
  1.4 0.0 copy-start.2
  1.4 0.0 copy-done.1
  1.4 0.7 %copy-done = s32[1,16,256]{2,1,0:T(8,128)S(1)} copy-done((s32[1,16,256]{2,1,0:T(8,128)S(1)}, s32[1,16,256]{2,1,0:T(8,128)}, u32[]{:S(2)}) %copy-start) | copy-done | bytes 16408
  2.1 0.0 copy-done.2
  2.1 62.2 %feti.1 = (f32[1,9,256]{2,1,0:T(8,128)S(1)}, f32[1,9,256]{2,1,0:T(8,128)S(1)}) custom-call(f32[1,9,256]{2,1,0:T(8,128)S(1)} %copy.7.mult_ref, f32[1,9,256]{2,1,0:T(8,128)S(1)} %copy.8.res_ref, s32[1,16,256]{2,1,0:T(8,128)S(1)} %copy-done, f32[8]{0:T(128)S(1)} %copy-done.2, f32[1,24,96]{2,1,0:T(8,128)S(1)} %copy-done.1), custom_call_target="tpu_custom_call" | custom-call | tf_op jit(solution)/shard_map/feti/pallas_call | solution.py:471
  64.3 0.6 copy.9
  64.9 0.6 copy.10
  (1 shorter events, 0.0 us)
Async XLA Ops:
  0.6 0.7 %copy-start.3 = (f32[1,9,256]{2,0,1:T(1,128)S(1)}, f32[1,9,256]{2,0,1:T(1,128)}, u32[]{:S(2)}) copy-start(f32[1,9,256]{2,0,1:T(1,128)} %param.6) | copy-start | bytes 27652
  0.6 0.7 %copy-start.1 = (f32[1,24,96]{2,1,0:T(8,128)S(1)}, f32[1,24,96]{2,1,0:T(8,128)}, u32[]{:S(2)}) copy-start(f32[1,24,96]{2,1,0:T(8,128)} %panel_ref.1) | copy-start | bytes 27652
  1.4 0.7 %copy-start = (s32[1,16,256]{2,1,0:T(8,128)S(1)}, s32[1,16,256]{2,1,0:T(8,128)}, u32[]{:S(2)}) copy-start(s32[1,16,256]{2,1,0:T(8,128)} %class_ref.1) | copy-start | bytes 49156
  1.4 0.7 %copy-start.2 = (f32[8]{0:T(128)S(1)}, f32[8]{0:T(128)}, u32[]{:S(2)}) copy-start(f32[8]{0:T(128)} %moduli_ref.1) | copy-start | bytes 100

commit v2 on v1

--- a/solution.py
+++ b/solution.py
@@ -155,45 +155,83 @@
     return t[:, 0:128] + t[:, 128:256]
 
 
-def eliminate(first, last, matrix):
-    size = matrix.shape[0]
-    row_a, lane_a = iota((size, 128), 0), iota((size, 128), 1)
-    row_b, lane_b = iota((8, 128), 0), iota((8, 128), 1)
-    lane_w = iota((1, 128), 1)
-
-    def block(k, a):
-        matrix[...] = a
-        base = pl.multiple_of(k * 8, 8)
-        b = matrix[pl.ds(base, 8), :]
-        local_a = row_a - base
-        for t in range(0, 8, 2):
-            r0, r1 = b[t : t + 1, :], b[t + 1 : t + 2, :]
-            p, q, s = r0[:, t : t + 1], r0[:, t + 1 : t + 2], r1[:, t + 1 : t + 2]
-            inverse = 1.0 / (p * s - q * q)
-            p, q, s = p * inverse, q * inverse, s * inverse
-            w0, w1 = s * r0 - q * r1, p * r1 - q * r0
-            w0 = jnp.where(lane_w == t, s, jnp.where(lane_w == t + 1, -q, w0))
-            w1 = jnp.where(lane_w == t, -q, jnp.where(lane_w == t + 1, p, w1))
-
-            def update(x, row, lane):
-                rows = x.shape[0]
-                column = row[:, 0:1]
-                c0 = jnp.where(column == t, -1.0, jnp.where(column == t + 1, 0.0, x[:, t : t + 1]))
-                c1 = jnp.where(column == t, 0.0, jnp.where(column == t + 1, -1.0, x[:, t + 1 : t + 2]))
-                hit = (row == t) | (row == t + 1) | (lane == t) | (lane == t + 1)
-                return jnp.where(hit, 0.0, x) - c0 * w0 - c1 * w1
-
-            a, b = update(a, local_a, lane_a), update(b, row_b, lane_b)
-        return roll(a, -8, 1)
-
-    matrix[...] = lax.fori_loop(first, last, block, matrix[...])
+def invert_columns(columns, row):
+    for t in range(0, 8, 2):
+        p, q = columns[t][t : t + 1], columns[t][t + 1 : t + 2]
+        s = columns[t + 1][t + 1 : t + 2]
+        d = 1.0 / p
+        e = q * d
+        p = 1.0 / (s - q * e)
+        q = e * p
+        s = d + e * q
+        pair = (row == t) | (row == t + 1)
+        c0 = jnp.where(pair, jnp.where(row == t, -1.0, 0.0), columns[t])
+        c1 = jnp.where(pair, jnp.where(row == t, 0.0, -1.0), columns[t + 1])
+        updated = []
+        for j in range(8):
+            if j == t:
+                base, w0, w1 = 0.0, s, -q
+            elif j == t + 1:
+                base, w0, w1 = 0.0, -q, p
+            else:
+                a, b = columns[j][t : t + 1], columns[j][t + 1 : t + 2]
+                base = jnp.where(pair, 0.0, columns[j])
+                w0, w1 = s * a - q * b, p * b - q * a
+            updated.append(base - c0 * w0 - c1 * w1)
+        columns = updated
+    return columns
+
+
+def eliminate(matrix):
+    count = matrix.shape[0] // 8
+    row, lane = iota((8, 128), 0), iota((8, 128), 1)
+    rows = [matrix[8 * i : 8 * i + 8, :] for i in range(count)]
+    for k in range(count):
+        pivot = rows[k]
+        first = 8 * k
+        columns = [
+            jnp.broadcast_to(pivot[:, first + t : first + t + 1], (8, 128)) for t in range(8)
+        ]
+        inverse = invert_columns(columns, row)
+        scaled = inverse[0] * pivot[0:1]
+        for t in range(1, 8):
+            scaled = scaled + inverse[t] * pivot[t : t + 1]
+        for t in range(8):
+            scaled = jnp.where(lane == first + t, inverse[t], scaled)
+        hit = (lane >= first) & (lane < first + 8)
+        for i in [(k + 1 + i) % count for i in range(count - 1)]:
+            change = None
+            for t in range(0, 8, 2):
+                c0 = rows[i][:, first + t : first + t + 1]
+                c1 = rows[i][:, first + t + 1 : first + t + 2]
+                term = c0 * scaled[t : t + 1] + c1 * scaled[t + 1 : t + 2]
+                change = term if change is None else change + term
+            rows[i] = jnp.where(hit, 0.0, rows[i]) - change
+        rows[k] = scaled
+    for i in range(count):
+        matrix[8 * i : 8 * i + 8, :] = rows[i]
 
 
 def kernel(
-    G, Y, Z, mult_ref, res_ref, class_ref, moduli_ref, panel_ref, lam_ref, out_ref,
-    matrix, panel, sent_hi, sent_lo, got_hi, got_lo, corner_out, corner_in,
-    tiles, x_in, yc_in, z_in, rows, send_sem, recv_sem,
+    G, Y, Z, mult_hbm, res_hbm, class_hbm, moduli_ref, panel_hbm, lam_ref, out_ref,
+    mult_ref, res_ref, class_ref, panel_ref, matrix, panel, sent_hi, sent_lo, got_hi,
+    got_lo, corner_out, corner_in, tiles, x_in, yc_in, z_in, rows, load_sem, send_sem,
+    recv_sem, far_sem,
 ):
+    loads = [
+        pltpu.make_async_copy(src, dst, load_sem.at[i])
+        for i, (src, dst) in enumerate(
+            (
+                (res_hbm, res_ref),
+                (panel_hbm, panel_ref),
+                (class_hbm, class_ref),
+                (mult_hbm, mult_ref),
+            )
+        )
+    ]
+    for load in loads:
+        load.start()
+
     sub, member = lax.axis_index("sub"), lax.axis_index("grp")
     n_sub = Y * Z * 2
     grid_row, grid_col = sub // SPAN, sub % SPAN
@@ -226,10 +264,14 @@
         for c in (1, 0)
         if (i, c) != (0, 0)
     ]
-    z_partners = [((y * Z + (z + i) % Z) * 2 + core, member) for i in by_distance(Z)]
+    along_z = lambda i: ((y * Z + (z + i) % Z) * 2 + core, member)
+    z_partners = [along_z(i) for i in by_distance(Z)]
 
     barrier = pltpu.get_barrier_semaphore()
-    greeted = z_partners + list(upper) + list(lower) + yc_partners + x_partners
+    greeted = [upper[0], lower[0], upper[1], lower[1]] + x_partners
+    greeted += [p for p in yc_partners if p is not yc_partners[-1]]
+    reach = min(2, Z // 2)
+    greeted += [along_z(i) for n in range(1, reach + 1) for i in (n, Z - n)]
     for device in greeted:
         pl.semaphore_signal(barrier, inc=1, device_id=device, device_id_type=MESH)
 
@@ -280,13 +322,16 @@
     size = G * CORNER
     own_rows = pl.ds(pl.multiple_of(member * CORNER, 8), CORNER)
     panel[...] = jnp.zeros((CORNER, 128), F32)
+    loads[1].wait()
     panel[:, 0:size] = panel_ref[0]
     matrix[own_rows, :] = panel[...]
 
+    loads[0].wait()
     residual = res_ref[0] * row_mask
     from_rows(residual, sent_hi.at[0])
     rows[0] = residual
 
+    loads[2].wait()
     classes = class_ref[0]
     stiffness = jnp.zeros((16, 256), F32)
     for level in range(8):
@@ -349,11 +394,18 @@
             for i, device in enumerate(x_partners)
         ]
 
-    def corner_field(e):
+    def corner_rhs(e):
         rhs = corner_out[e]
         for i in range(G - 1):
             rhs = rhs + corner_in[e, i]
-        rhs = jnp.sum(rhs, axis=0, keepdims=True)
+        return jnp.sum(rhs, axis=0, keepdims=True)
+
+    row_m, lane_m = iota((size, 128), 0), iota((size, 128), 1)
+
+    def as_column(line):
+        return jnp.sum(jnp.where(row_m == lane_m, line, 0.0), axis=1, keepdims=True)
+
+    def corner_field(rhs):
         solved = jnp.sum(matrix[own_rows, :] * rhs, axis=1, keepdims=True)
         parts = []
         for c in range(3):
@@ -363,10 +415,18 @@
             parts.append((1.0 - ramp_x) * t0 + ramp_x * t1)
         return jnp.concatenate(parts, axis=0)
 
+    def far_signal(distance, slot):
+        for i in (distance, Z - distance):
+            pl.semaphore_signal(
+                far_sem.at[slot], inc=1, device_id=along_z(i), device_id_type=MESH
+            )
+
     pl.semaphore_wait(barrier, len(greeted))
 
     group = exchange(0, both=False)
     panels = [send(panel, matrix.at[own_rows, :], device) for device in x_partners]
+    if Z > 4:
+        far_signal(2, 0)
     wait(group)
     f_r = place(sent_hi[0], got_hi[0] * low_mask)
 
@@ -375,23 +435,26 @@
     pack(image, sent_lo.at[1], False)
     group = exchange(1)
     dots = [0.25 * partial_dot(f_r, image)]
+    if Z > 4:
+        pl.semaphore_wait(far_sem.at[0], 2)
+        if Z > 8:
+            far_signal(4, 1)
     wait(panels)
-    half = size // 16
-    eliminate(0, half, matrix)
+    eliminate(matrix)
     wait(group)
     u = (sent_hi[1] - got_lo[1]) * (0.25 * up_mask)
     f_u = place(u, (got_hi[1] - sent_lo[1]) * (0.25 * low_mask))
 
     group = corner_send(0, f_u)
     v = vcycle(f_u)
-    eliminate(half, 2 * half, matrix)
-    matrix[...] = roll(matrix[...], size - 128, 1)
     wait(group)
-    v = v + corner_field(0)
+    rhs_u = corner_rhs(0)
+    v = v + corner_field(rhs_u)
     pack(v, sent_hi.at[2], True)
     pack(v, sent_lo.at[2], False)
     group = exchange(2)
     dots.append(partial_dot(f_u, v))
+    column_u = as_column(rhs_u)
     to_rows(u, rows, 1)
     wait(group)
     q = (sent_hi[2] - got_lo[2]) * up_mask
@@ -403,47 +466,55 @@
     group = exchange(3)
     dots.append(0.25 * partial_dot(f_r, image))
     dots.append(0.25 * partial_dot(f_q, image))
+    if Z > 8:
+        pl.semaphore_wait(far_sem.at[1], 2)
     to_rows(q, rows, 2)
     wait(group)
     w = (sent_hi[3] - got_lo[3]) * (0.25 * up_mask)
     f_w = place(w, (got_hi[3] - sent_lo[3]) * (0.25 * low_mask))
 
-    group = corner_send(1, f_w)
-    v = vcycle(f_w)
-    wait(group)
-    v = v + corner_field(1)
-    dots.append(partial_dot(f_u, v))
-    dots.append(partial_dot(f_w, v))
-
-    tile = jnp.zeros((8, 128), F32)
-    for i, d in enumerate(dots):
-        tile = tile + jnp.where(row8 == i, d, 0.0)
-
-    def spread(slot, landing, partners):
+    def spread(slot, tile, landing, partners):
         tiles[slot] = tile
         return [
             send(tiles.at[slot], landing.at[i], device) for i, device in enumerate(partners)
         ]
 
-    def collect(group, landing):
+    def collect(group, tile, landing):
         wait(group)
-        total = tile
         for i in range(landing.shape[0]):
-            total = total + landing[i]
-        return total
-
-    group = spread(0, x_in, x_partners)
+            tile = tile + landing[i]
+        return tile
+
+    corners = corner_send(1, f_w)
+    v = vcycle(f_w)
+    dots.append(partial_dot(f_u, v))
+    dots.append(partial_dot(f_w, v))
+    tile = jnp.zeros((8, 128), F32)
+    for i, d in enumerate(dots):
+        tile = tile + jnp.where(row8 == i, d, 0.0)
+    group = spread(0, tile, x_in, x_partners)
+    wait(corners)
+    rhs_w = corner_rhs(1)
+    solved_w = jnp.sum(matrix[...] * rhs_w, axis=1, keepdims=True)
+    coarse_us = jnp.sum(column_u * solved_w, axis=0, keepdims=True)
+    coarse_ws = jnp.sum(as_column(rhs_w) * solved_w, axis=0, keepdims=True)
+    coarse = jnp.where(row8 == 4, coarse_us, jnp.where(row8 == 5, coarse_ws, 0.0))
+    tile = tile + jnp.where(lane8 == 0, coarse, 0.0)
+    tile = collect(group, tile, x_in)
+    group = spread(1, tile, yc_in, yc_partners)
+    v = v + corner_field(rhs_w)
     pack(v, sent_hi.at[4], True)
     pack(v, sent_lo.at[4], False)
     last = exchange(4, up=False)
     to_rows(w, rows, 3)
-    tile = collect(group, x_in)
-    group = spread(1, yc_in, yc_partners)
+    tile = collect(group, tile, yc_in)
+    group = spread(2, tile, z_in, z_partners)
     wait(last)
     to_rows((sent_hi[4] - got_lo[4]) * up_mask, rows, 4)
-    tile = collect(group, yc_in)
-    group = spread(2, z_in, z_partners)
-    tile = collect(group, z_in)
+    loads[3].wait()
+    for copy in copies:
+        copy.wait_send()
+    tile = collect(group, tile, z_in)
 
     sums = jnp.sum(tile, axis=1, keepdims=True)
     ru, uq, rw, qw, us, ws = [sums[i : i + 1, :] for i in range(6)]
@@ -455,8 +526,6 @@
     first, second = a + b * c, a * b
     lam_ref[0] = mult_ref[0] * row_mask + first * rows[1] - second * rows[3]
     out_ref[0] = rows[0] - first * rows[2] + second * rows[4]
-    for copy in copies:
-        copy.wait_send()
 
 
 def solution(mesh):
@@ -468,12 +537,17 @@
 
     def per_device(multipliers, residual, stiff_class, moduli, coarse_panel):
         vmem = pl.BlockSpec(memory_space=pltpu.VMEM)
+        hbm = pl.BlockSpec(memory_space=pl.ANY)
         return pl.pallas_call(
             functools.partial(kernel, G, Y, Z),
             out_shape=[jax.ShapeDtypeStruct((1, 9, 256), F32)] * 2,
-            in_specs=[vmem, vmem, vmem, pl.BlockSpec(memory_space=pltpu.SMEM), vmem],
+            in_specs=[hbm, hbm, hbm, pl.BlockSpec(memory_space=pltpu.SMEM), hbm],
             out_specs=[vmem, vmem],
             scratch_shapes=[
+                pltpu.VMEM((1, 9, 256), F32),
+                pltpu.VMEM((1, 9, 256), F32),
+                pltpu.VMEM((1, 16, 256), jnp.int32),
+                pltpu.VMEM((1, CORNER, size), F32),
                 pltpu.VMEM((size, 128), F32),
                 pltpu.VMEM((CORNER, 128), F32),
                 pltpu.VMEM((5, 40, 128), F32),
@@ -487,8 +561,10 @@
                 pltpu.VMEM((2 * Y - 1, 8, 128), F32),
                 pltpu.VMEM((Z - 1, 8, 128), F32),
                 pltpu.VMEM((5, 9, 256), F32),
+                pltpu.SemaphoreType.DMA((4,)),
                 pltpu.SemaphoreType.DMA((copies,)),
                 pltpu.SemaphoreType.DMA((copies,)),
+                pltpu.SemaphoreType.REGULAR((2,)),
             ],
             compiler_params=pltpu.CompilerParams(
                 collective_id=0, has_side_effects=True, vmem_limit_bytes=32 * 1024 * 1024

time: 65.8 us -> 55 us (0.84)
  Pallas kernels: 62.2 us -> 51.4 us
    pallas_call x1, Pallas kernels: 62.2 us -> 51.4 us  [per_device(): pl.pallas_call(functools.partial(kernel, G, Y, Z), out_shape=[jax.ShapeDt...]
where the time goes in v2:
time: 55 us; the launch traced here: 54.7 us
  Pallas kernels  51.4 us (93%)
  local copies, waits for them, and re-layouts  2.64 us (5%)
  between operations  0.68 us (1%)
    pallas_call x1, Pallas kernels, per_device(): pl.pallas_call(functools.partial(kernel, G, Y, Z), out_shape=[jax.ShapeDt...  51.4 us
    unnamed x10, local copies, waits for them, and re-layouts  1.42 us
    pallas_call x2, local copies, waits for them, and re-layouts, per_device(): pl.pallas_call(functools.partial(kernel, G, Y, Z), out_shape=[jax.ShapeDt...  1.22 us

profile of v2, /device:TPU:1, one launch (start us, length us, event | category | flops | bytes accessed | tf_op | source)
XLA Modules:
  0.0 54.7 jit_solution(484595625520183697)
XLA Ops:
  0.6 0.0 copy-start.3
  0.6 0.0 copy-start.1
  0.6 0.7 %copy.7.mult_hbm = f32[1,9,256]{2,1,0:T(8,128)S(1)} copy(f32[1,9,256]{2,0,1:T(1,128)} %param.5) | data formatting | bytes 18432 | tf_op args[0]
  1.4 0.0 copy-done.3
  1.4 0.0 copy-start
  1.4 0.0 copy-start.2
  1.4 0.0 copy-done.1
  1.4 0.7 %copy-done = s32[1,16,256]{2,1,0:T(8,128)S(1)} copy-done((s32[1,16,256]{2,1,0:T(8,128)S(1)}, s32[1,16,256]{2,1,0:T(8,128)}, u32[]{:S(2)}) %copy-start) | copy-done | bytes 16408
  2.1 0.0 copy-done.2
  2.1 51.4 %feti.1 = (f32[1,9,256]{2,1,0:T(8,128)S(1)}, f32[1,9,256]{2,1,0:T(8,128)S(1)}) custom-call(f32[1,9,256]{2,1,0:T(8,128)S(1)} %copy.7.mult_hbm, f32[1,9,256]{2,1,0:T(8,128)S(1)} %copy.8.res_hbm, s32[1,16,256]{2,1,0:T(8,128)S(1)} %copy-done, f32[8]{0:T(128)S(1)} %copy-done.2, f32[1,24,96]{2,1,0:T(8,128)S(1)} %copy-done.1), custom_call_target="tpu_custom_call" | custom-call | tf_op jit(solution)/shard_map/feti/pallas_call | solution.py:541
  53.5 0.6 %copy.9 = f32[1,9,256]{2,0,1:T(1,128)} copy(f32[1,9,256]{2,1,0:T(8,128)S(1)} %get-tuple-element.2) | data formatting | bytes 18432 | tf_op jit(solution)/shard_map/feti/pallas_call | solution.py:541
  54.1 0.6 %copy.10 = f32[1,9,256]{2,0,1:T(1,128)} copy(f32[1,9,256]{2,1,0:T(8,128)S(1)} %get-tuple-element.3) | data formatting | bytes 18432 | tf_op jit(solution)/shard_map/feti/pallas_call | solution.py:541
  (1 shorter events, 0.0 us)
Async XLA Ops:
  0.6 0.7 %copy-start.3 = (f32[1,9,256]{2,0,1:T(1,128)S(1)}, f32[1,9,256]{2,0,1:T(1,128)}, u32[]{:S(2)}) copy-start(f32[1,9,256]{2,0,1:T(1,128)} %param.6) | copy-start | bytes 27652
  0.6 0.7 %copy-start.1 = (f32[1,24,96]{2,1,0:T(8,128)S(1)}, f32[1,24,96]{2,1,0:T(8,128)}, u32[]{:S(2)}) copy-start(f32[1,24,96]{2,1,0:T(8,128)} %panel_hbm.1) | copy-start | bytes 27652
  1.4 0.7 %copy-start = (s32[1,16,256]{2,1,0:T(8,128)S(1)}, s32[1,16,256]{2,1,0:T(8,128)}, u32[]{:S(2)}) copy-start(s32[1,16,256]{2,1,0:T(8,128)} %class_hbm.1) | copy-start | bytes 49156
  1.4 0.7 %copy-start.2 = (f32[8]{0:T(128)S(1)}, f32[8]{0:T(128)}, u32[]{:S(2)}) copy-start(f32[8]{0:T(128)} %moduli_ref.1) | copy-start | bytes 100

commit v3 on v2

--- a/solution.py
+++ b/solution.py
@@ -213,8 +213,8 @@
 
 
 def kernel(
-    G, Y, Z, mult_hbm, res_hbm, class_hbm, moduli_ref, panel_hbm, lam_ref, out_ref,
-    mult_ref, res_ref, class_ref, panel_ref, matrix, panel, sent_hi, sent_lo, got_hi,
+    G, Y, Z, mult_hbm, res_hbm, class_hbm, moduli_hbm, panel_hbm, lam_ref, out_ref,
+    mult_ref, res_ref, class_ref, moduli_ref, panel_ref, matrix, panel, sent_hi, sent_lo, got_hi,
     got_lo, corner_out, corner_in, tiles, x_in, yc_in, z_in, rows, load_sem, send_sem,
     recv_sem, far_sem,
 ):
@@ -226,11 +226,11 @@
                 (panel_hbm, panel_ref),
                 (class_hbm, class_ref),
                 (mult_hbm, mult_ref),
+                (moduli_hbm, moduli_ref),
             )
         )
     ]
-    for load in loads:
-        load.start()
+    loads[0].start()
 
     sub, member = lax.axis_index("sub"), lax.axis_index("grp")
     n_sub = Y * Z * 2
@@ -275,6 +275,9 @@
     for device in greeted:
         pl.semaphore_signal(barrier, inc=1, device_id=device, device_id_type=MESH)
 
+    for load in loads[1:]:
+        load.start()
+
     copies = []
 
     def send(src, dst, device):
@@ -327,11 +330,12 @@
     matrix[own_rows, :] = panel[...]
 
     loads[0].wait()
-    residual = res_ref[0] * row_mask
+    residual = res_ref[:, 0, :] * row_mask
     from_rows(residual, sent_hi.at[0])
     rows[0] = residual
 
     loads[2].wait()
+    loads[4].wait()
     classes = class_ref[0]
     stiffness = jnp.zeros((16, 256), F32)
     for level in range(8):
@@ -385,7 +389,7 @@
             s = jnp.sum(s[:, 0:128] + s[:, 128:256], axis=1, keepdims=True)
             at = (lane8 == member * CORNER + row8 * 4 + n) & (row8 < 6)
             result = result + jnp.where(at, s, 0.0)
-        return result
+        return jnp.sum(result, axis=0, keepdims=True)
 
     def corner_send(e, f):
         corner_out[e] = corner_sums(f)
@@ -398,7 +402,16 @@
         rhs = corner_out[e]
         for i in range(G - 1):
             rhs = rhs + corner_in[e, i]
-        return jnp.sum(rhs, axis=0, keepdims=True)
+        return rhs
+
+    lane1 = iota((1, 128), 1)
+
+    def summed(products):
+        t = jnp.zeros((8, 128), F32)
+        for i, d in products:
+            t = t + jnp.where(row8 == i, d, 0.0)
+        t = jnp.sum(t, axis=1, keepdims=True)
+        return jnp.sum(jnp.where(row8 == lane8, t, 0.0), axis=0, keepdims=True)
 
     row_m, lane_m = iota((size, 128), 0), iota((size, 128), 1)
 
@@ -468,6 +481,7 @@
     dots.append(0.25 * partial_dot(f_q, image))
     if Z > 8:
         pl.semaphore_wait(far_sem.at[1], 2)
+    early = summed(list(enumerate(dots)))
     to_rows(q, rows, 2)
     wait(group)
     w = (sent_hi[3] - got_lo[3]) * (0.25 * up_mask)
@@ -487,19 +501,15 @@
 
     corners = corner_send(1, f_w)
     v = vcycle(f_w)
-    dots.append(partial_dot(f_u, v))
-    dots.append(partial_dot(f_w, v))
-    tile = jnp.zeros((8, 128), F32)
-    for i, d in enumerate(dots):
-        tile = tile + jnp.where(row8 == i, d, 0.0)
+    tile = early + summed([(4, partial_dot(f_u, v)), (5, partial_dot(f_w, v))])
     group = spread(0, tile, x_in, x_partners)
     wait(corners)
     rhs_w = corner_rhs(1)
     solved_w = jnp.sum(matrix[...] * rhs_w, axis=1, keepdims=True)
     coarse_us = jnp.sum(column_u * solved_w, axis=0, keepdims=True)
     coarse_ws = jnp.sum(as_column(rhs_w) * solved_w, axis=0, keepdims=True)
-    coarse = jnp.where(row8 == 4, coarse_us, jnp.where(row8 == 5, coarse_ws, 0.0))
-    tile = tile + jnp.where(lane8 == 0, coarse, 0.0)
+    coarse = jnp.where(lane1 == 4, coarse_us, jnp.where(lane1 == 5, coarse_ws, 0.0))
+    tile = tile + coarse
     tile = collect(group, tile, x_in)
     group = spread(1, tile, yc_in, yc_partners)
     v = v + corner_field(rhs_w)
@@ -516,16 +526,15 @@
         copy.wait_send()
     tile = collect(group, tile, z_in)
 
-    sums = jnp.sum(tile, axis=1, keepdims=True)
-    ru, uq, rw, qw, us, ws = [sums[i : i + 1, :] for i in range(6)]
+    ru, uq, rw, qw, us, ws = [tile[:, i : i + 1] for i in range(6)]
     a = ru / uq
     next_inner = ru - a * (rw + uq) + a * a * qw
     c = 1.0 + next_inner / ru
     curve = c * c * uq - c * a * (us + qw) + a * a * ws
     b = next_inner / curve
     first, second = a + b * c, a * b
-    lam_ref[0] = mult_ref[0] * row_mask + first * rows[1] - second * rows[3]
-    out_ref[0] = rows[0] - first * rows[2] + second * rows[4]
+    lam_ref[:, 0, :] = mult_ref[:, 0, :] * row_mask + first * rows[1] - second * rows[3]
+    out_ref[:, 0, :] = rows[0] - first * rows[2] + second * rows[4]
 
 
 def solution(mesh):
@@ -537,16 +546,19 @@
 
     def per_device(multipliers, residual, stiff_class, moduli, coarse_panel):
         vmem = pl.BlockSpec(memory_space=pltpu.VMEM)
-        hbm = pl.BlockSpec(memory_space=pl.ANY)
-        return pl.pallas_call(
+        hbm = pl.BlockSpec(memory_space=pltpu.HBM)
+        face_first = (1, 0, 2)
+        in_hbm = lambda x: pltpu.with_memory_space_constraint(x, pltpu.HBM)
+        lam, out = pl.pallas_call(
             functools.partial(kernel, G, Y, Z),
-            out_shape=[jax.ShapeDtypeStruct((1, 9, 256), F32)] * 2,
-            in_specs=[hbm, hbm, hbm, pl.BlockSpec(memory_space=pltpu.SMEM), hbm],
+            out_shape=[jax.ShapeDtypeStruct((9, 1, 256), F32)] * 2,
+            in_specs=[hbm] * 5,
             out_specs=[vmem, vmem],
             scratch_shapes=[
-                pltpu.VMEM((1, 9, 256), F32),
-                pltpu.VMEM((1, 9, 256), F32),
+                pltpu.VMEM((9, 1, 256), F32),
+                pltpu.VMEM((9, 1, 256), F32),
                 pltpu.VMEM((1, 16, 256), jnp.int32),
+                pltpu.SMEM((8,), F32),
                 pltpu.VMEM((1, CORNER, size), F32),
                 pltpu.VMEM((size, 128), F32),
                 pltpu.VMEM((CORNER, 128), F32),
@@ -554,14 +566,14 @@
                 pltpu.VMEM((5, 40, 128), F32),
                 pltpu.VMEM((5, 40, 128), F32),
                 pltpu.VMEM((5, 40, 128), F32),
-                pltpu.VMEM((2, 8, 128), F32),
-                pltpu.VMEM((2, G - 1, 8, 128), F32),
-                pltpu.VMEM((3, 8, 128), F32),
-                pltpu.VMEM((G - 1, 8, 128), F32),
-                pltpu.VMEM((2 * Y - 1, 8, 128), F32),
-                pltpu.VMEM((Z - 1, 8, 128), F32),
+                pltpu.VMEM((2, 1, 128), F32),
+                pltpu.VMEM((2, G - 1, 1, 128), F32),
+                pltpu.VMEM((3, 1, 128), F32),
+                pltpu.VMEM((G - 1, 1, 128), F32),
+                pltpu.VMEM((2 * Y - 1, 1, 128), F32),
+                pltpu.VMEM((Z - 1, 1, 128), F32),
                 pltpu.VMEM((5, 9, 256), F32),
-                pltpu.SemaphoreType.DMA((4,)),
+                pltpu.SemaphoreType.DMA((5,)),
                 pltpu.SemaphoreType.DMA((copies,)),
                 pltpu.SemaphoreType.DMA((copies,)),
                 pltpu.SemaphoreType.REGULAR((2,)),
@@ -570,7 +582,14 @@
                 collective_id=0, has_side_effects=True, vmem_limit_bytes=32 * 1024 * 1024
             ),
             name="feti",
-        )(multipliers, residual, stiff_class, moduli, coarse_panel)
+        )(
+            in_hbm(multipliers.transpose(face_first)),
+            in_hbm(residual.transpose(face_first)),
+            in_hbm(stiff_class),
+            in_hbm(moduli),
+            in_hbm(coarse_panel),
+        )
+        return lam.transpose(face_first), out.transpose(face_first)
 
     device = P(("sub", "grp"), None, None)
     return jax.shard_map(

time: 55 us -> 51.6 us (0.938)
  Pallas kernels: 51.4 us -> 49.6 us
  local copies, waits for them, and re-layouts: 2.64 us -> 1.2 us
    pallas_call x1, Pallas kernels: 51.4 us -> 49.6 us  [per_device(): pl.pallas_call(functools.partial(kernel, G, Y, Z), out_shape=[jax.ShapeDt...]
    pallas_call x2 -> x0, local copies, waits for them, and re-layouts: 1.22 us -> none  [per_device(): pl.pallas_call(functools.partial(kernel, G, Y, Z), out_shape=[jax.ShapeDt...]
    unnamed x10 -> x2, local copies, waits for them, and re-layouts: 1.42 us -> 1.2 us
where the time goes in v3:
time: 51.6 us; the launch traced here: 51.4 us
  Pallas kernels  49.6 us (96%)
  local copies, waits for them, and re-layouts  1.2 us (2%)
  between operations  0.64 us (1%)
    pallas_call x1, Pallas kernels, per_device(): pl.pallas_call(functools.partial(kernel, G, Y, Z), out_shape=[jax.ShapeDt...  49.6 us
    unnamed x2, local copies, waits for them, and re-layouts  1.2 us

profile of v3, /device:TPU:1, one launch (start us, length us, event | category | flops | bytes accessed | tf_op | source)
XLA Modules:
  0.0 51.4 jit_solution(4928650882895983988)
XLA Ops:
  0.6 49.6 %feti.1 = (f32[9,1,256]{2,1,0:T(1,128)S(1)}, f32[9,1,256]{2,1,0:T(1,128)S(1)}) custom-call(f32[9,1,256]{2,1,0:T(1,128)} %bitcast.6, f32[9,1,256]{2,1,0:T(1,128)} %bitcast.7, s32[1,16,256]{2,1,0:T(8,128)} %class_hbm.1, f32[8]{0:T(128)} %moduli_hbm.1, f32[1,24,96]{2,1,0:T(8,128)} %panel_hbm.1), custom_call_target="tpu_custom_call" | custom-call | tf_op jit(solution)/shard_map/feti/pallas_call | solution.py:552
  50.2 0.6 %copy.9 = f32[1,9,256]{2,0,1:T(1,128)} copy(f32[1,9,256]{2,0,1:T(1,128)S(1)} %bitcast.5) | data formatting | bytes 18432
  50.8 0.6 %copy.10 = f32[1,9,256]{2,0,1:T(1,128)} copy(f32[1,9,256]{2,0,1:T(1,128)S(1)} %bitcast.4) | data formatting | bytes 18432

commit v4 on v3

--- a/solution.py
+++ b/solution.py
@@ -215,7 +215,7 @@
 def kernel(
     G, Y, Z, mult_hbm, res_hbm, class_hbm, moduli_hbm, panel_hbm, lam_ref, out_ref,
     mult_ref, res_ref, class_ref, moduli_ref, panel_ref, matrix, panel, sent_hi, sent_lo, got_hi,
-    got_lo, corner_out, corner_in, tiles, x_in, yc_in, z_in, rows, load_sem, send_sem,
+    got_lo, corner_out, corner_in, tiles, x_in, sub_in, rows, load_sem, sum_sem, send_sem,
     recv_sem, far_sem,
 ):
     loads = [
@@ -265,7 +265,12 @@
         if (i, c) != (0, 0)
     ]
     along_z = lambda i: ((y * Z + (z + i) % Z) * 2 + core, member)
-    z_partners = [along_z(i) for i in by_distance(Z)]
+    distance = lambda o: min(o[0], Y - o[0]) + min(o[1], Z - o[1])
+    offsets = [(i, j, c) for i in range(Y) for j in range(Z) for c in range(2)][1:]
+    sub_partners = [
+        (((y + i) % Y * Z + (z + j) % Z) * 2 + (core + c) % 2, member)
+        for i, j, c in sorted(offsets, key=distance, reverse=True)
+    ]
 
     barrier = pltpu.get_barrier_semaphore()
     greeted = [upper[0], lower[0], upper[1], lower[1]] + x_partners
@@ -352,15 +357,18 @@
     def operator(v):
         return m3(diagonal, v) - weighted(weight, v, 1)
 
-    def vcycle(f):
+    def before_correction(f):
         g = m3(scale, f)
-        v = g
-        v = (1.0 - DAMP) * v + g + weighted(relax, v, 1)
-        h = m3(coarse_scale, pair_sum(f - operator(v)))
+        v = (1.0 - DAMP) * g + g + weighted(relax, g, 1)
+        defect = f - operator(v)
+        h = m3(coarse_scale, pair_sum(defect))
         e = h
         for _ in range(3):
             e = (1.0 - DAMP) * e + h + weighted(coarse_relax, e, 2)
-        v = v + e
+        return v, defect, v + e
+
+    def after_correction(f, v):
+        g = m3(scale, f)
         for _ in range(2):
             v = (1.0 - DAMP) * v + g + weighted(relax, v, 1)
         return v
@@ -428,18 +436,21 @@
             parts.append((1.0 - ramp_x) * t0 + ramp_x * t1)
         return jnp.concatenate(parts, axis=0)
 
-    def far_signal(distance, slot):
-        for i in (distance, Z - distance):
+    def far_signal(slot):
+        step = min((1, 3, 4)[slot], Z // 2 - 1)
+        for i in (step, Z - step):
             pl.semaphore_signal(
                 far_sem.at[slot], inc=1, device_id=along_z(i), device_id_type=MESH
             )
 
+    def far_wait(slot):
+        pl.semaphore_wait(far_sem.at[slot], 2)
+
     pl.semaphore_wait(barrier, len(greeted))
 
     group = exchange(0, both=False)
     panels = [send(panel, matrix.at[own_rows, :], device) for device in x_partners]
-    if Z > 4:
-        far_signal(2, 0)
+    far_signal(0)
     wait(group)
     f_r = place(sent_hi[0], got_hi[0] * low_mask)
 
@@ -448,10 +459,8 @@
     pack(image, sent_lo.at[1], False)
     group = exchange(1)
     dots = [0.25 * partial_dot(f_r, image)]
-    if Z > 4:
-        pl.semaphore_wait(far_sem.at[0], 2)
-        if Z > 8:
-            far_signal(4, 1)
+    far_wait(0)
+    far_signal(1)
     wait(panels)
     eliminate(matrix)
     wait(group)
@@ -459,7 +468,8 @@
     f_u = place(u, (got_hi[1] - sent_lo[1]) * (0.25 * low_mask))
 
     group = corner_send(0, f_u)
-    v = vcycle(f_u)
+    _, defect_u, v = before_correction(f_u)
+    v = after_correction(f_u, v)
     wait(group)
     rhs_u = corner_rhs(0)
     v = v + corner_field(rhs_u)
@@ -467,6 +477,8 @@
     pack(v, sent_lo.at[2], False)
     group = exchange(2)
     dots.append(partial_dot(f_u, v))
+    far_wait(1)
+    far_signal(2)
     column_u = as_column(rhs_u)
     to_rows(u, rows, 1)
     wait(group)
@@ -479,52 +491,63 @@
     group = exchange(3)
     dots.append(0.25 * partial_dot(f_r, image))
     dots.append(0.25 * partial_dot(f_q, image))
-    if Z > 8:
-        pl.semaphore_wait(far_sem.at[1], 2)
+    far_wait(2)
     early = summed(list(enumerate(dots)))
     to_rows(q, rows, 2)
     wait(group)
     w = (sent_hi[3] - got_lo[3]) * (0.25 * up_mask)
     f_w = place(w, (got_hi[3] - sent_lo[3]) * (0.25 * low_mask))
 
-    def spread(slot, tile, landing, partners):
-        tiles[slot] = tile
-        return [
-            send(tiles.at[slot], landing.at[i], device) for i, device in enumerate(partners)
+    corners = corner_send(1, f_w)
+    before, defect_w, after = before_correction(f_w)
+    tile = early + summed(
+        [
+            (4, partial_dot(f_u, before) + partial_dot(defect_u, after)),
+            (5, partial_dot(f_w, before) + partial_dot(defect_w, after)),
         ]
-
-    def collect(group, tile, landing):
-        wait(group)
-        for i in range(landing.shape[0]):
-            tile = tile + landing[i]
-        return tile
-
-    corners = corner_send(1, f_w)
-    v = vcycle(f_w)
-    tile = early + summed([(4, partial_dot(f_u, v)), (5, partial_dot(f_w, v))])
-    group = spread(0, tile, x_in, x_partners)
+    )
+    tiles[0] = tile
+    group = [
+        send(tiles.at[0], x_in.at[i], device) for i, device in enumerate(x_partners)
+    ]
+    v = after_correction(f_w, after)
     wait(corners)
     rhs_w = corner_rhs(1)
+    v = v + corner_field(rhs_w)
+    pack(v, sent_lo.at[4], False)
+    last = exchange(4, up=False)
     solved_w = jnp.sum(matrix[...] * rhs_w, axis=1, keepdims=True)
     coarse_us = jnp.sum(column_u * solved_w, axis=0, keepdims=True)
     coarse_ws = jnp.sum(as_column(rhs_w) * solved_w, axis=0, keepdims=True)
     coarse = jnp.where(lane1 == 4, coarse_us, jnp.where(lane1 == 5, coarse_ws, 0.0))
     tile = tile + coarse
-    tile = collect(group, tile, x_in)
-    group = spread(1, tile, yc_in, yc_partners)
-    v = v + corner_field(rhs_w)
+    wait(group)
+    for i in range(G - 1):
+        tile = tile + x_in[i]
+
+    tiles[1] = tile
+    for i, device in enumerate(sub_partners):
+        pltpu.make_async_remote_copy(
+            src_ref=tiles.at[1], dst_ref=sub_in.at[i], send_sem=sum_sem.at[0],
+            recv_sem=sum_sem.at[1], device_id=device, device_id_type=MESH,
+        ).start()
+    arrived = pltpu.make_async_remote_copy(
+        src_ref=sub_in, dst_ref=sub_in, send_sem=sum_sem.at[0], recv_sem=sum_sem.at[1],
+        device_id=sub_partners[0], device_id_type=MESH,
+    )
     pack(v, sent_hi.at[4], True)
-    pack(v, sent_lo.at[4], False)
-    last = exchange(4, up=False)
     to_rows(w, rows, 3)
-    tile = collect(group, tile, yc_in)
-    group = spread(2, tile, z_in, z_partners)
     wait(last)
     to_rows((sent_hi[4] - got_lo[4]) * up_mask, rows, 4)
     loads[3].wait()
     for copy in copies:
         copy.wait_send()
-    tile = collect(group, tile, z_in)
+    arrived.wait_recv()
+    parts = [sub_in[i] for i in range(len(sub_partners))] + [tile]
+    while len(parts) > 1:
+        parts = [sum(parts[i : i + 2][1:], parts[i]) for i in range(0, len(parts), 2)]
+    tile = parts[0]
+    arrived.wait_send()
 
     ru, uq, rw, qw, us, ws = [tile[:, i : i + 1] for i in range(6)]
     a = ru / uq
@@ -542,7 +565,7 @@
     Z = min(16, n_sub // 2)
     Y = n_sub // (2 * Z)
     size = G * CORNER
-    copies = 3 + 3 * 6 + 3 + 4 * (G - 1) + (2 * Y - 1) + (Z - 1)
+    copies = 3 + 3 * 6 + 3 + 4 * (G - 1)
 
     def per_device(multipliers, residual, stiff_class, moduli, coarse_panel):
         vmem = pl.BlockSpec(memory_space=pltpu.VMEM)
@@ -568,15 +591,15 @@
                 pltpu.VMEM((5, 40, 128), F32),
                 pltpu.VMEM((2, 1, 128), F32),
                 pltpu.VMEM((2, G - 1, 1, 128), F32),
-                pltpu.VMEM((3, 1, 128), F32),
+                pltpu.VMEM((2, 1, 128), F32),
                 pltpu.VMEM((G - 1, 1, 128), F32),
-                pltpu.VMEM((2 * Y - 1, 1, 128), F32),
-                pltpu.VMEM((Z - 1, 1, 128), F32),
+                pltpu.VMEM((n_sub - 1, 1, 128), F32),
                 pltpu.VMEM((5, 9, 256), F32),
                 pltpu.SemaphoreType.DMA((5,)),
+                pltpu.SemaphoreType.DMA((2,)),
                 pltpu.SemaphoreType.DMA((copies,)),
                 pltpu.SemaphoreType.DMA((copies,)),
-                pltpu.SemaphoreType.REGULAR((2,)),
+                pltpu.SemaphoreType.REGULAR((3,)),
             ],
             compiler_params=pltpu.CompilerParams(
                 collective_id=0, has_side_effects=True, vmem_limit_bytes=32 * 1024 * 1024

time: 51.6 us -> 50.7 us (0.983)
  Pallas kernels: 49.6 us -> 48.7 us
    pallas_call x1, Pallas kernels: 49.6 us -> 48.7 us  [per_device(): pl.pallas_call(functools.partial(kernel, G, Y, Z), out_shape=[jax.ShapeDt...]
where the time goes in v4:
time: 50.7 us; the launch traced here: 50.5 us
  Pallas kernels  48.7 us (96%)
  local copies, waits for them, and re-layouts  1.2 us (2%)
  between operations  0.64 us (1%)
    pallas_call x1, Pallas kernels, per_device(): pl.pallas_call(functools.partial(kernel, G, Y, Z), out_shape=[jax.ShapeDt...  48.7 us
    unnamed x2, local copies, waits for them, and re-layouts  1.2 us

profile of v4, /device:TPU:1, one launch (start us, length us, event | category | flops | bytes accessed | tf_op | source)
XLA Modules:
  0.0 50.5 jit_solution(12489618091224996291)
XLA Ops:
  0.6 48.7 %feti.1 = (f32[9,1,256]{2,1,0:T(1,128)S(1)}, f32[9,1,256]{2,1,0:T(1,128)S(1)}) custom-call(f32[9,1,256]{2,1,0:T(1,128)} %bitcast.6, f32[9,1,256]{2,1,0:T(1,128)} %bitcast.7, s32[1,16,256]{2,1,0:T(8,128)} %class_hbm.1, f32[8]{0:T(128)} %moduli_hbm.1, f32[1,24,96]{2,1,0:T(8,128)} %panel_hbm.1), custom_call_target="tpu_custom_call" | custom-call | tf_op jit(solution)/shard_map/feti/pallas_call | solution.py:575
  49.3 0.6 %copy.9 = f32[1,9,256]{2,0,1:T(1,128)} copy(f32[1,9,256]{2,0,1:T(1,128)S(1)} %bitcast.5) | data formatting | bytes 18432
  49.9 0.6 %copy.10 = f32[1,9,256]{2,0,1:T(1,128)} copy(f32[1,9,256]{2,0,1:T(1,128)S(1)} %bitcast.4) | data formatting | bytes 18432

commit v5 on v4

--- a/solution.py
+++ b/solution.py
@@ -85,16 +85,25 @@
     return jnp.concatenate(parts, axis=0)
 
 
-def pack(v, buf, high):
+def pack_first(v, buf, high, lines=None):
+    at = 15 if high else 0
+    for c in range(3):
+        row = v[16 * c + at : 16 * c + at + 1, :]
+        if lines is not None:
+            row = row + lines[c]
+        buf[c : c + 1, :] = row[:, 0:128]
+        buf[3 + c : 4 + c, :] = row[:, 128:256]
+    buf[6:8, :] = jnp.zeros((2, 128), F32)
+
+
+def pack_rest(v, buf, high):
     lane = iota((16, 128), 1)
     inner = lane % 16
     at = 15 if high else 0
     y = z = None
     for c in range(3):
         for h in range(2):
-            r = 3 * h + c
             part = v[16 * c : 16 * c + 16, 128 * h : 128 * h + 128]
-            buf[r : r + 1, :] = part[at : at + 1, :]
             t = roll(jnp.where(inner == at, part, 0.0), c + 3 * h - at, 1)
             z = t if z is None else z + t
         if high:
@@ -104,7 +113,6 @@
             part = v[16 * c : 16 * c + 16, 0:128]
             t = roll(jnp.where(lane < 16, part, 0.0), 16 * c, 1)
         y = t if y is None else y + t
-    buf[6:8, :] = jnp.zeros((2, 128), F32)
     buf[8:24, :] = y
     buf[24:40, :] = z
 
@@ -300,9 +308,8 @@
             copy.wait_recv()
 
     spans = ((0, 8), (8, 24), (24, 40))
-    order = (0, 2, 1)
-
-    def exchange(e, both=True, up=True):
+
+    def exchange(e, both=True, up=True, order=(0, 2, 1)):
         group = []
         for k in order:
             first, last = spans[k]
@@ -426,15 +433,29 @@
     def as_column(line):
         return jnp.sum(jnp.where(row_m == lane_m, line, 0.0), axis=1, keepdims=True)
 
-    def corner_field(rhs):
+    def corner_lines(rhs):
         solved = jnp.sum(matrix[own_rows, :] * rhs, axis=1, keepdims=True)
-        parts = []
+        first, last = [], []
         for c in range(3):
             t = solved[8 * c : 8 * c + 8] * plane8
-            t0 = jnp.sum(jnp.where(row8w < 4, t, 0.0), axis=0, keepdims=True)
-            t1 = jnp.sum(jnp.where(row8w >= 4, t, 0.0), axis=0, keepdims=True)
-            parts.append((1.0 - ramp_x) * t0 + ramp_x * t1)
+            first.append(jnp.sum(jnp.where(row8w < 4, t, 0.0), axis=0, keepdims=True))
+            last.append(jnp.sum(jnp.where(row8w >= 4, t, 0.0), axis=0, keepdims=True))
+        return first, last
+
+    def corner_field(first, last):
+        parts = [(1.0 - ramp_x) * a + ramp_x * b for a, b in zip(first, last)]
         return jnp.concatenate(parts, axis=0)
+
+    def layers(e, v, corners=None):
+        first, last = (None, None) if corners is None else corners
+        pack_first(v, sent_hi.at[e], True, last)
+        pack_first(v, sent_lo.at[e], False, first)
+        group = exchange(e, order=(0,))
+        if corners is not None:
+            v = v + corner_field(first, last)
+        pack_rest(v, sent_hi.at[e], True)
+        pack_rest(v, sent_lo.at[e], False)
+        return group + exchange(e, order=(2, 1)), v
 
     def far_signal(slot):
         step = min((1, 3, 4)[slot], Z // 2 - 1)
@@ -455,9 +476,7 @@
     f_r = place(sent_hi[0], got_hi[0] * low_mask)
 
     image = operator(f_r)
-    pack(image, sent_hi.at[1], True)
-    pack(image, sent_lo.at[1], False)
-    group = exchange(1)
+    group, _ = layers(1, image)
     dots = [0.25 * partial_dot(f_r, image)]
     far_wait(0)
     far_signal(1)
@@ -472,10 +491,7 @@
     v = after_correction(f_u, v)
     wait(group)
     rhs_u = corner_rhs(0)
-    v = v + corner_field(rhs_u)
-    pack(v, sent_hi.at[2], True)
-    pack(v, sent_lo.at[2], False)
-    group = exchange(2)
+    group, v = layers(2, v, corner_lines(rhs_u))
     dots.append(partial_dot(f_u, v))
     far_wait(1)
     far_signal(2)
@@ -486,9 +502,7 @@
     f_q = place(q, (got_hi[2] - sent_lo[2]) * low_mask)
 
     image = operator(f_q)
-    pack(image, sent_hi.at[3], True)
-    pack(image, sent_lo.at[3], False)
-    group = exchange(3)
+    group, _ = layers(3, image)
     dots.append(0.25 * partial_dot(f_r, image))
     dots.append(0.25 * partial_dot(f_q, image))
     far_wait(2)
@@ -513,8 +527,9 @@
     v = after_correction(f_w, after)
     wait(corners)
     rhs_w = corner_rhs(1)
-    v = v + corner_field(rhs_w)
-    pack(v, sent_lo.at[4], False)
+    v = v + corner_field(*corner_lines(rhs_w))
+    pack_first(v, sent_lo.at[4], False)
+    pack_rest(v, sent_lo.at[4], False)
     last = exchange(4, up=False)
     solved_w = jnp.sum(matrix[...] * rhs_w, axis=1, keepdims=True)
     coarse_us = jnp.sum(column_u * solved_w, axis=0, keepdims=True)
@@ -535,7 +550,8 @@
         src_ref=sub_in, dst_ref=sub_in, send_sem=sum_sem.at[0], recv_sem=sum_sem.at[1],
         device_id=sub_partners[0], device_id_type=MESH,
     )
-    pack(v, sent_hi.at[4], True)
+    pack_first(v, sent_hi.at[4], True)
+    pack_rest(v, sent_hi.at[4], True)
     to_rows(w, rows, 3)
     wait(last)
     to_rows((sent_hi[4] - got_lo[4]) * up_mask, rows, 4)
@@ -558,6 +574,17 @@
     first, second = a + b * c, a * b
     lam_ref[:, 0, :] = mult_ref[:, 0, :] * row_mask + first * rows[1] - second * rows[3]
     out_ref[:, 0, :] = rows[0] - first * rows[2] + second * rows[4]
+
+
+def deliver(lam_ref, out_ref, lam_hbm, out_hbm, sem):
+    copies = [
+        pltpu.make_async_copy(lam_ref, lam_hbm, sem.at[0]),
+        pltpu.make_async_copy(out_ref, out_hbm, sem.at[1]),
+    ]
+    for copy in copies:
+        copy.start()
+    for copy in copies:
+        copy.wait()
 
 
 def solution(mesh):
@@ -612,6 +639,15 @@
             in_hbm(moduli),
             in_hbm(coarse_panel),
         )
+        lam, out = pl.pallas_call(
+            deliver,
+            out_shape=[jax.ShapeDtypeStruct((9, 1, 256), F32)] * 2,
+            in_specs=[vmem, vmem],
+            out_specs=[hbm, hbm],
+            scratch_shapes=[pltpu.SemaphoreType.DMA((2,))],
+            compiler_params=pltpu.CompilerParams(vmem_limit_bytes=1024 * 1024),
+            name="deliver",
+        )(lam, out)
         return lam.transpose(face_first), out.transpose(face_first)
 
     device = P(("sub", "grp"), None, None)

time: 50.7 us -> 49.9 us (0.984)
  local copies, waits for them, and re-layouts: 1.2 us -> 0 us
    unnamed x2 -> x0, local copies, waits for them, and re-layouts: 1.2 us -> none
    pallas_call x0 -> x1, Pallas kernels: none -> 0.62 us  [per_device(): pl.pallas_call(deliver, out_shape=[jax.ShapeDtypeStruct((9, 1, 256), F32)...]
where the time goes in v5:
time: 49.9 us; the launch traced here: 49.7 us
  Pallas kernels  49.1 us (98%)
  between operations  0.64 us (1%)
    pallas_call x1, Pallas kernels, per_device(): pl.pallas_call(functools.partial(kernel, G, Y, Z), out_shape=[jax.ShapeDt...  48.5 us

profile of v5, /device:TPU:1, one launch (start us, length us, event | category | flops | bytes accessed | tf_op | source)
XLA Modules:
  0.0 49.7 jit_solution(4272927774074678816)
XLA Ops:
  0.6 48.5 %feti.1 = (f32[9,1,256]{2,1,0:T(1,128)S(1)}, f32[9,1,256]{2,1,0:T(1,128)S(1)}) custom-call(f32[9,1,256]{2,1,0:T(1,128)} %bitcast.4, f32[9,1,256]{2,1,0:T(1,128)} %bitcast.5, s32[1,16,256]{2,1,0:T(8,128)} %class_hbm.1, f32[8]{0:T(128)} %moduli_hbm.1, f32[1,24,96]{2,1,0:T(8,128)} %panel_hbm.1), custom_call_target="tpu_custom_call" | custom-call | tf_op jit(solution)/shard_map/feti/pallas_call | solution.py:602
  49.1 0.6 %deliver.1 = (f32[9,1,256]{2,1,0:T(1,128)}, f32[9,1,256]{2,1,0:T(1,128)}) custom-call(f32[9,1,256]{2,1,0:T(1,128)S(1)} %get-tuple-element.6.lam_ref, f32[9,1,256]{2,1,0:T(1,128)S(1)} %get-tuple-element.7.out_ref), custom_call_target="tpu_custom_call" | custom-call | tf_op jit(solution)/shard_map/deliver/pallas_call | solution.py:642

commit v6 on v5

--- a/solution.py
+++ b/solution.py
@@ -487,7 +487,7 @@
     f_u = place(u, (got_hi[1] - sent_lo[1]) * (0.25 * low_mask))
 
     group = corner_send(0, f_u)
-    _, defect_u, v = before_correction(f_u)
+    _, _, v = before_correction(f_u)
     v = after_correction(f_u, v)
     wait(group)
     rhs_u = corner_rhs(0)
@@ -495,7 +495,6 @@
     dots.append(partial_dot(f_u, v))
     far_wait(1)
     far_signal(2)
-    column_u = as_column(rhs_u)
     to_rows(u, rows, 1)
     wait(group)
     q = (sent_hi[2] - got_lo[2]) * up_mask
@@ -516,7 +515,7 @@
     before, defect_w, after = before_correction(f_w)
     tile = early + summed(
         [
-            (4, partial_dot(f_u, before) + partial_dot(defect_u, after)),
+            (4, jnp.sum(q * w, axis=0, keepdims=True)),
             (5, partial_dot(f_w, before) + partial_dot(defect_w, after)),
         ]
     )
@@ -527,21 +526,20 @@
     v = after_correction(f_w, after)
     wait(corners)
     rhs_w = corner_rhs(1)
-    v = v + corner_field(*corner_lines(rhs_w))
-    pack_first(v, sent_lo.at[4], False)
-    pack_rest(v, sent_lo.at[4], False)
-    last = exchange(4, up=False)
     solved_w = jnp.sum(matrix[...] * rhs_w, axis=1, keepdims=True)
-    coarse_us = jnp.sum(column_u * solved_w, axis=0, keepdims=True)
     coarse_ws = jnp.sum(as_column(rhs_w) * solved_w, axis=0, keepdims=True)
-    coarse = jnp.where(lane1 == 4, coarse_us, jnp.where(lane1 == 5, coarse_ws, 0.0))
-    tile = tile + coarse
+    tile = tile + jnp.where(lane1 == 5, coarse_ws, 0.0)
     wait(group)
     for i in range(G - 1):
         tile = tile + x_in[i]
 
     tiles[1] = tile
     for i, device in enumerate(sub_partners):
+        if i == len(sub_partners) // 4:
+            v = v + corner_field(*corner_lines(rhs_w))
+            pack_first(v, sent_lo.at[4], False)
+            pack_rest(v, sent_lo.at[4], False)
+            last = exchange(4, up=False)
         pltpu.make_async_remote_copy(
             src_ref=tiles.at[1], dst_ref=sub_in.at[i], send_sem=sum_sem.at[0],
             recv_sem=sum_sem.at[1], device_id=device, device_id_type=MESH,

time: 49.9 us -> 49.9 us (level)
  no operation moved by 1% of the time
where the time goes in v6:
time: 49.9 us; the launch traced here: 49.7 us
  Pallas kernels  49.1 us (98%)
  between operations  0.64 us (1%)
    pallas_call x1, Pallas kernels, per_device(): pl.pallas_call(functools.partial(kernel, G, Y, Z), out_shape=[jax.ShapeDt...  48.5 us

profile of v6, /device:TPU:1, one launch (start us, length us, event | category | flops | bytes accessed | tf_op | source)
XLA Modules:
  0.0 49.7 jit_solution(14713014478118151603)
XLA Ops:
  0.6 48.5 %feti.1 = (f32[9,1,256]{2,1,0:T(1,128)S(1)}, f32[9,1,256]{2,1,0:T(1,128)S(1)}) custom-call(f32[9,1,256]{2,1,0:T(1,128)} %bitcast.4, f32[9,1,256]{2,1,0:T(1,128)} %bitcast.5, s32[1,16,256]{2,1,0:T(8,128)} %class_hbm.1, f32[8]{0:T(128)} %moduli_hbm.1, f32[1,24,96]{2,1,0:T(8,128)} %panel_hbm.1), custom_call_target="tpu_custom_call" | custom-call | tf_op jit(solution)/shard_map/feti/pallas_call | solution.py:600
  49.1 0.6 %deliver.1 = (f32[9,1,256]{2,1,0:T(1,128)}, f32[9,1,256]{2,1,0:T(1,128)}) custom-call(f32[9,1,256]{2,1,0:T(1,128)S(1)} %get-tuple-element.6.lam_ref, f32[9,1,256]{2,1,0:T(1,128)S(1)} %get-tuple-element.7.out_ref), custom_call_target="tpu_custom_call" | custom-call | tf_op jit(solution)/shard_map/deliver/pallas_call | solution.py:640
